TPU v7x, 256 devices: a whole 4x4x8 slice. The times are simulated.
256 devices in a mesh: batch: 16 (over z, core), tm: 16 (over x, y).
Axes of the slice: x: 4, y: 4, z: 8, core: 2. Of those that a mesh axis runs over, the one named last changes fastest.
Arguments:
- feat_a: bfloat16 [16, 16, 4096, 256], P('batch', 'tm'), may hold values from -6 to 6
- feat_b: bfloat16 [16, 16, 4096, 256], P('batch', 'tm'), may hold values from -6 to 6
- flow_in_weight: float32 [128, 81], replicated, may hold values from -0.625 to 0.625
- flow_entry_bias: float32 [128], replicated, may hold values from -3 to 3
- flow_out_weight: float32 [3, 3, 2, 128], replicated, may hold values from -0.1875 to 0.1875
- frame_mix: float32 [16, 16], replicated, may hold values from -1.5 to 1.5
- expand_weight: bfloat16 [256, 1024], replicated, may hold values from -1.5 to 1.5
- expand_bias: float32 [1024], replicated, may hold values from -3 to 3
Outputs:
- flow: float32 [16, 16, 2, 4096], P('batch', 'tm')
- cov_grad: bfloat16 [2, 16, 16, 256, 1024], P(None, 'batch', None, 'tm')
All inputs are finite; a program needn't handle non-finite values.
Results may differ from a plain program's by a relative error of at most 0.0061.
Values may be sent and summed in bfloat16 or wider, within the bound.
A program may use at most 192 MiB of HBM per device.

v0:
```python
import math

import jax
import jax.numpy as jnp
from jax import lax
from jax.sharding import PartitionSpec as P

HF = 64
WF = 64
D_FEAT = 256
EXP = 1024
DEC = 128
RADIUS = 4
POOLED = 256


def passed_along(value, axis, steps):
    count = lax.axis_size(axis)
    first, last = (max(0, -steps), min(count, count - steps))
    return lax.ppermute(value, axis, [(source, source + steps) for source in range(first, last)])


def banded_volume(first, latter_item):
    span = 2 * RADIUS + 1
    border_filled = jnp.pad(latter_item, ((RADIUS, RADIUS), (0, 0), (0, 0)))
    products = jnp.stack(
        [
            jnp.einsum(
                "hxc,hyc->hxy",
                first,
                border_filled[shift : shift + HF],
                preferred_element_type=jnp.float32,
            )
            for shift in range(span)
        ]
    )
    col_ids = lax.broadcasted_iota(jnp.int32, (span, WF, WF), 1)
    row_ids = lax.broadcasted_iota(jnp.int32, (span, WF, WF), 2)
    offsets = lax.broadcasted_iota(jnp.int32, (span, WF, WF), 0)
    band = (row_ids == col_ids + offsets - RADIUS).astype(jnp.float32)
    corr = jnp.einsum("ahxy,bxy->abhx", products, band, precision=lax.Precision.HIGHEST)
    return corr.reshape(span * span, HF * WF) / math.sqrt(D_FEAT)


def decode(corr, flow_in_weight, flow_entry_bias, flow_out_weight):
    top_precision = lax.Precision.HIGHEST
    hidden = jax.nn.gelu(
        jnp.dot(flow_in_weight, corr, precision=top_precision) + flow_entry_bias[:, None]
    )
    border_filled = jnp.pad(hidden.reshape(DEC, HF, WF), ((0, 0), (1, 1), (1, 1)))
    output = jnp.zeros((2, HF * WF), jnp.float32)
    for row_tap in range(3):
        for column_offset in range(3):
            window = border_filled[
                :, row_tap : row_tap + HF, column_offset : column_offset + WF
            ].reshape(DEC, HF * WF)
            output = output + jnp.dot(
                flow_out_weight[row_tap, column_offset], window, precision=top_precision
            )
    return output


def pool_local(feat):
    clips = feat.shape[0]
    blocks = feat.reshape(clips, 1, HF // 4, 4, WF // 4, 4, D_FEAT)
    pooled = jnp.mean(blocks, axis=(3, 5), dtype=jnp.float32)
    return pooled.reshape(clips, 1, POOLED, D_FEAT).astype(jnp.bfloat16)


def on_device(
    feat_a,
    feat_b,
    flow_in_weight,
    flow_entry_bias,
    flow_out_weight,
    frame_mix,
    expand_weight,
    expand_bias,
):
    top_precision = lax.Precision.HIGHEST
    clips = feat_a.shape[0]
    following = passed_along(feat_a, "tm", -1)
    firsts = feat_a.reshape(clips, HF, WF, D_FEAT)
    seconds = following.reshape(clips, HF, WF, D_FEAT)

    def one_pair(pair):
        corr = banded_volume(pair[0], pair[1])
        return decode(corr, flow_in_weight, flow_entry_bias, flow_out_weight)

    flow = lax.map(one_pair, (firsts, seconds)).reshape(clips, 1, 2, HF * WF)

    def expand(regrouped):
        count = regrouped.shape[0]
        frames = regrouped.shape[1]
        block = regrouped.shape[2]
        mixed = jnp.einsum(
            "gf,kfqd->kgqd", frame_mix, regrouped.astype(jnp.float32), precision=top_precision
        ).astype(jnp.bfloat16)
        embed = (
            jnp.dot(mixed.reshape(-1, D_FEAT), expand_weight, preferred_element_type=jnp.float32)
            + expand_bias
        )
        return jax.nn.gelu(embed).astype(jnp.bfloat16).reshape(count, frames, block, EXP)

    embed_a = expand(
        lax.all_to_all(pool_local(feat_a), "tm", split_axis=2, concat_axis=1, tiled=True)
    )
    embed_b = expand(
        lax.all_to_all(pool_local(feat_b), "tm", split_axis=2, concat_axis=1, tiled=True)
    )
    frames = embed_a.shape[1]
    block = embed_a.shape[2]
    stacked = jnp.stack([embed_a.reshape(-1, EXP), embed_b.reshape(-1, EXP)])
    local_sums = jnp.sum(stacked, axis=1, dtype=jnp.float32)
    gram = jnp.einsum("vrk,vrj->vkj", stacked, stacked, preferred_element_type=jnp.float32)
    total_sums = lax.psum(local_sums, ("batch", "tm"))
    rows_total = stacked.shape[1] * lax.axis_size("batch") * lax.axis_size("tm")
    mean_removed = stacked.astype(jnp.float32) - (total_sums / rows_total)[:, None, :]
    grad_scale = 1.0 / math.sqrt(EXP)
    partial_block = lax.psum_scatter(gram, "tm", scatter_dimension=2, tiled=True)
    summed_block = lax.psum(partial_block, "batch")
    piece = lax.all_gather(summed_block, "tm", axis=2, tiled=True)
    width = piece.shape[2]
    covariance_matrix = (piece - total_sums[:, :, None] * total_sums[:, None, :] / rows_total) / (
        rows_total - 1
    )
    row_ids = lax.broadcasted_iota(jnp.int32, (EXP, width), 0)
    col_ids = lax.broadcasted_iota(jnp.int32, (EXP, width), 1)
    covariance_matrix = jnp.where((row_ids == col_ids)[None], 0.0, covariance_matrix)
    gradient_list = (
        jnp.einsum("mha,maq->mhq", mean_removed, covariance_matrix, precision=top_precision)
        * grad_scale
    )
    cov_grad = gradient_list.astype(jnp.bfloat16).reshape(2, clips, frames, block, EXP)
    return (flow, cov_grad)


def solution(mesh):
    return jax.shard_map(
        on_device,
        mesh=mesh,
        in_specs=(
            P("batch", "tm", None, None),
            P("batch", "tm", None, None),
            P(),
            P(),
            P(),
            P(),
            P(),
            P(),
        ),
        out_specs=(P("batch", "tm", None, None), P(None, "batch", None, "tm", None)),
        check_vma=False,
    )
```

profile of v0, /device:TPU:1, one launch (start us, length us, event | category | flops | bytes accessed | tf_op | source)
XLA Modules:
  0.0 550.4 jit_solution(16339481567889954369)
XLA Ops:
  8.6 4.6 reshape.189
  13.2 3.7 reduce_sum.27
  19.8 9.5 %all-to-all-start = ((bf16[16,2,2048]{2,1,0:T(2,128)(2,1)}), bf16[16,2,2048]{2,1,0:T(2,128)(2,1)S(1)}, u32[]{:S(2)}, u32[]{:S(2)}) async-start(bf16[16,2,2048]{2,1,0:T(2,128)(2,1)} %reshape.196), calls=%async_computation | async-start | bytes 262144 | tf_op jit(solution)/shard_map/all_to_all | solution.py:106
  29.3 2.8 reshape.190
  32.2 3.5 reduce_sum.28
  38.1 22.4 %all-to-all-done = bf16[16,2,2048]{2,1,0:T(2,128)(2,1)S(1)} async-done(((bf16[16,2,2048]{2,1,0:T(2,128)(2,1)}), bf16[16,2,2048]{2,1,0:T(2,128)(2,1)S(1)}, u32[]{:S(2)}, u32[]{:S(2)}) %all-to-all-start) | async-done | bytes 131104 | tf_op jit(solution)/shard_map/all_to_all | solution.py:106
  60.5 7.5 %all-to-all-start.1 = ((bf16[16,2,2048]{2,1,0:T(2,128)(2,1)}), bf16[16,2,2048]{2,1,0:T(2,128)(2,1)S(1)}, u32[]{:S(2)}, u32[]{:S(2)}) async-start(bf16[16,2,2048]{2,1,0:T(2,128)(2,1)} %reshape.194), calls=%async_computation.1 | async-start | bytes 262144 | tf_op jit(solution)/shard_map/all_to_all | solution.py:109
  71.0 3.7 all-to-all-done.1
  76.5 79.0 %psum.14 = f32[2,1024]{1,0:T(2,128)S(1)} all-reduce(f32[2,1024]{1,0:T(2,128)S(1)} %convert_reduce_fusion), channel_id=1, replica_groups=mesh['batch'=16,'tm'=16] {'batch','tm'}, use_global_device_ids=true, to_apply=%region_3.4 | all-reduce | flops 2048 | bytes 16384 | tf_op jit(solution)/shard_map/psum | solution.py:116
  157.9 12.9 %copy.43 = f32[2,1024,1024]{1,0,2:T(2,128)} copy(f32[2,1024,1024]{1,2,0:T(8,128)S(1)} %fusion.36) | data formatting | bytes 16777216 | tf_op jit(solution)/shard_map/vrk,vrj->vkj/dot_general | solution.py:115
  172.4 3.6 bitcast_dynamic-update-slice_fusion.7
  176.0 3.6 bitcast_dynamic-update-slice_fusion.6
  179.6 3.6 bitcast_dynamic-update-slice_fusion.5
  183.2 3.6 bitcast_dynamic-update-slice_fusion.4
  186.9 130.8 %all-reduce.8.cloned.1.call-done = f32[2,1024,1024]{1,0,2:T(2,128)} async-done(((f32[2,1024,1024]{1,0,2:T(2,128)}), f32[2,1024,1024]{1,0,2:T(2,128)}) %all-reduce.8.cloned.1.call-update) | async-done | bytes 8388624
  317.7 1.9 constant_dynamic-slice_fusion
  319.7 3.6 bitcast_dynamic-update-slice_fusion.8
  323.3 105.7 %all-reduce.6.cloned.1.call-done = f32[2,1024,64]{1,0,2:T(2,128)} async-done(((f32[2,1024,64]{1,0,2:T(2,128)}), f32[2,1024,64]{1,0,2:T(2,128)}) %all-reduce.6.cloned.1.call-update) | async-done | bytes 524304 | tf_op jit(solution)/shard_map/psum | solution.py:121
  429.1 3.6 bitcast_dynamic-update-slice_fusion.3
  432.7 3.6 bitcast_dynamic-update-slice_fusion.2
  436.2 3.6 bitcast_dynamic-update-slice_fusion.1
  439.8 3.6 bitcast_dynamic-update-slice_fusion
  443.5 20.2 %copy.34 = f32[9,64,64,64]{3,1,0,2:T(8,128)} copy(f32[9,64,64,64]{2,3,1,0:T(8,128)} %bitcast_dynamic-update-slice_fusion) | data formatting | bytes 18874368 | tf_op jit(solution)/shard_map/while/body/eval_jaxpr/stack | solution.py:26
  463.6 26.5 %multiply_bitcast_fusion = f32[9,9,64,64]{2,1,0,3:T(8,128)} fusion(f32[9,64,64,64]{3,1,0,2:T(8,128)} %copy.34), kind=kOutput, calls=%fused_computation.5 | convolution fusion | flops 255246336 | bytes 10764288 | tf_op jit(solution)/shard_map/while/body/eval_jaxpr/ahxy,bxy->abhx/dot_general | solution.py:41
  490.1 3.6 copy.35
  493.8 2.0 div.34
  495.8 5.1 fusion.10
  500.9 4.0 pad_slice_fusion
  518.1 2.1 convolution_add_fusion.2
  520.1 2.5 fusion.3
  522.7 10.7 %multiply_select_fusion = f32[2,1024,1024]{1,0,2:T(2,128)S(1)} fusion(f32[2,1024,1024]{1,0,2:T(2,128)} %all-gather.2.cloned.1.call-done, pred[1024,1024]{0,1:T(8,128)(4,1)S(1)} %copy-done.7, f32[2,1024]{0,1:T(8,128)S(1)} %copy-done.9, f32[2,1024]{1,0:T(2,128)S(1)} %copy-done.11), kind=kLoop, calls=%fused_computation.2 | loop fusion | flops 10485760 | bytes 17842176 | tf_op jit(solution)/shard_map/jit(_where)/select_n | solution.py:129
  533.4 10.2 %multiply_convert_fusion = bf16[2,256,1024]{2,1,0:T(8,128)(2,1)} fusion(f32[2,1024,1024]{1,0,2:T(2,128)S(1)} %multiply_select_fusion, f32[2,1024]{1,0:T(2,128)S(1)} %copy-done.12, bf16[1,256,1024]{2,1,0:T(8,128)(2,1)S(1)} %copy-done.6, bf16[1,256,1024]{2,1,0:T(8,128)(2,1)S(1)} %copy-done.4), kind=kOutput, calls=%fused_computation.43 | convolution fusion | flops 6445072384 | bytes 10493952 | tf_op jit(solution)/shard_map/mha,maq->mhq/dot_general | solution.py:131
  (79 shorter events, 27.9 us)
Async XLA Ops:
  7.2 68.0 %copy-start = (bf16[256,1024]{1,0:T(8,128)(2,1)S(1)}, bf16[256,1024]{1,0:T(8,128)(2,1)}, u32[]{:S(2)}) copy-start(bf16[256,1024]{1,0:T(8,128)(2,1)} %param.14) | copy-start | bytes 1572868
  7.2 164.3 %collective-permute-start = (bf16[1,1,4096,256]{3,2,1,0:T(8,128)(2,1)}, bf16[1,1,4096,256]{3,2,1,0:T(8,128)(2,1)}, u32[]{:S(2)}, u32[]{:S(2)}) collective-permute-start(bf16[1,1,4096,256]{3,2,1,0:T(8,128)(2,1)} %param.8), channel_id=1, source_target_pairs={{1,0},{2,1},{3,2},{4,3},{5,4},{6,5},{7,6},{8,7},{9,8},{10,9},{11,1... | collective-permute-start | bytes 6291464 | tf_op jit(solution)/shard_map/ppermute | solution.py:20
  13.2 16.1 %copy-start.8 = (bf16[1,1,4096,256]{3,2,1,0:T(8,128)(2,1)S(1)}, bf16[1,1,4096,256]{3,2,1,0:T(8,128)(2,1)}, u32[]{:S(2)}) copy-start(bf16[1,1,4096,256]{3,2,1,0:T(8,128)(2,1)} %param.9) | copy-start | bytes 6291460
  19.8 40.8 %all-to-all-start = ((bf16[16,2,2048]{2,1,0:T(2,128)(2,1)}), bf16[16,2,2048]{2,1,0:T(2,128)(2,1)S(1)}, u32[]{:S(2)}, u32[]{:S(2)}) async-start(bf16[16,2,2048]{2,1,0:T(2,128)(2,1)} %reshape.196), calls=%async_computation | async-start | bytes 262144 | tf_op jit(solution)/shard_map/all_to_all | solution.py:106
  35.7 33.6 %copy-start.18 = (u32[256]{0:T(256)S(1)}, u32[256]{0:T(256)}, u32[]{:S(2)}) copy-start(u32[256]{0:T(256)} %constant.62) | copy-start | bytes 3076
  35.7 35.0 %copy-start.13 = (f32[16,16]{1,0:T(8,128)S(1)}, f32[16,16]{1,0:T(8,128)}, u32[]{:S(2)}) copy-start(f32[16,16]{1,0:T(8,128)} %param.13) | copy-start | bytes 3076
  37.4 37.8 %copy-start.16 = (f32[1024]{0:T(1024)S(1)}, f32[1024]{0:T(1024)}, u32[]{:S(2)}) copy-start(f32[1024]{0:T(1024)} %param.15) | copy-start | bytes 12292
  60.5 14.2 %all-to-all-start.1 = ((bf16[16,2,2048]{2,1,0:T(2,128)(2,1)}), bf16[16,2,2048]{2,1,0:T(2,128)(2,1)S(1)}, u32[]{:S(2)}, u32[]{:S(2)}) async-start(bf16[16,2,2048]{2,1,0:T(2,128)(2,1)} %reshape.194), calls=%async_computation.1 | async-start | bytes 262144 | tf_op jit(solution)/shard_map/all_to_all | solution.py:109
  68.0 249.7 %all-reduce.8.cloned.1.call-start = ((), (), s32[]{:S(2)}) async-start(), calls=%async_computation.4 | async-start | bytes 16777216
  75.7 80.8 %copy-start.3 = (bf16[1,256,1024]{2,1,0:T(8,128)(2,1)}, bf16[1,256,1024]{2,1,0:T(8,128)(2,1)S(1)}, u32[]{:S(2)}) copy-start(bf16[1,256,1024]{2,1,0:T(8,128)(2,1)S(1)} %fusion.23) | copy-start | bytes 1572868
  76.3 81.6 %copy-start.5 = (bf16[1,256,1024]{2,1,0:T(8,128)(2,1)}, bf16[1,256,1024]{2,1,0:T(8,128)(2,1)S(1)}, u32[]{:S(2)}) copy-start(bf16[1,256,1024]{2,1,0:T(8,128)(2,1)S(1)} %fusion.32) | copy-start | bytes 1572868
  155.5 15.4 %copy-start.10 = (f32[2,1024]{1,0:T(2,128)}, f32[2,1024]{1,0:T(2,128)S(1)}, u32[]{:S(2)}) copy-start(f32[2,1024]{1,0:T(2,128)S(1)} %psum.14) | copy-start | bytes 24580
  170.8 1.6 copy-start.2
  170.8 258.2 %all-reduce.6.cloned.1.call-start = ((), (), s32[]{:S(2)}) async-start(), calls=%async_computation.2 | async-start | bytes 1048576 | tf_op jit(solution)/shard_map/psum | solution.py:121
  319.6 203.0 %all-gather.2.cloned.1.call-start = ((), (), s32[]{:S(2)}) async-start(), calls=%async_computation.3 | async-start | bytes 8912896 | tf_op jit(solution)/shard_map/all_gather | solution.py:122
  493.7 2.0 copy-start.15
  493.7 2.0 copy-start.17
  500.9 4.0 copy-start.14
  518.0 4.6 copy-start.7
  518.0 4.6 copy-start.9
  518.0 4.6 copy-start.11
  522.6 10.8 %copy-start.4 = (bf16[1,256,1024]{2,1,0:T(8,128)(2,1)S(1)}, bf16[1,256,1024]{2,1,0:T(8,128)(2,1)}, u32[]{:S(2)}) copy-start(bf16[1,256,1024]{2,1,0:T(8,128)(2,1)} %copy-done.3) | copy-start | bytes 1572868
  522.6 10.8 %copy-start.6 = (bf16[1,256,1024]{2,1,0:T(8,128)(2,1)S(1)}, bf16[1,256,1024]{2,1,0:T(8,128)(2,1)}, u32[]{:S(2)}) copy-start(bf16[1,256,1024]{2,1,0:T(8,128)(2,1)} %copy-done.5) | copy-start | bytes 1572868
  522.6 10.8 %copy-start.12 = (f32[2,1024]{1,0:T(2,128)S(1)}, f32[2,1024]{1,0:T(2,128)}, u32[]{:S(2)}) copy-start(f32[2,1024]{1,0:T(2,128)} %broadcast_multiply_fusion) | copy-start | bytes 24580
  533.4 10.3 %copy-start.1 = (bf16[256,1024]{1,0:T(8,128)(2,1)S(1)}, bf16[256,1024]{1,0:T(8,128)(2,1)}, u32[]{:S(2)}) copy-start(bf16[256,1024]{1,0:T(8,128)(2,1)} %param.14) | copy-start | bytes 1572868
Sparse Core Ops, SparseCore 0:
  171.0 146.6 all-reduce.7
  320.1 108.8 all-reduce.5
  431.5 76.1 all-gather.1
where the time goes:
time: 558 us; the launch traced here: 550 us
  waiting for transfers between devices  263 us (47%)
  matrix products  94.9 us (17%)
  blocking collectives  79 us (14%)
  local copies, waits for them, and re-layouts  57.4 us (10%)
  other arithmetic  22.9 us (4%)
  starting transfers between devices  18.6 us (3%)
  between operations  15 us (3%)
    unnamed x4, waiting for transfers between devices  131 us
    psum x1, waiting for transfers between devices, on_device(): summed_block = lax.psum(partial_block, 'batch')  106 us
    psum x1, blocking collectives, on_device(): total_sums = lax.psum(local_sums, ('batch', 'tm'))  79 us
    dot_general x9, matrix products, banded_volume(): jnp.einsum('hxc,hyc->hxy', first, border_filled[shift:shift + HF], prefer...  32.5 us
    dot_general x1, matrix products, banded_volume(): jnp.einsum('ahxy,bxy->abhx', products, band, precision=lax.Precision.HIGH...  26.5 us
    all_to_all x1, waiting for transfers between devices, on_device(): lax.all_to_all(pool_local(feat_a), 'tm', split_axis=2, concat_axis=1, til...  22.4 us
    another operation x1, local copies, waits for them, and re-layouts, banded_volume(): jnp.stack([jnp.einsum('hxc,hyc->hxy', first, border_filled[shift:shift +...  20.2 us
    dot_general x9, matrix products, decode(): jnp.dot(flow_out_weight[row_tap, column_offset], window, precision=top_pr...  17.7 us
  transfers between devices with their start and end apart: 6, of which 4 were waited for; matrix products, arithmetic and copies ran while one was open for 27% of the time, Pallas kernels for 0%

commit v1 on v0

v1 whole, which is shorter than its diff:
```python
import functools
import math

import jax
import jax.numpy as jnp
from jax import lax
from jax.experimental import pallas as pl
from jax.experimental.pallas import tpu as pltpu
from jax.sharding import PartitionSpec as P

MESH = pl.DeviceIdType.MESH
F32 = jnp.float32
BF16 = jnp.bfloat16

HF = 64
WF = 64
D_FEAT = 256
EXP = 1024
HALF = EXP // 2
DEC = 128
DISP = 81
POSITIONS = HF * WF
POOLED = 256
GROUP = 4 * WF
TASK = 32 * WF
REACH = 4 * WF
NEXT_ROWS = TASK + 2 * REACH
STRIP = 34 * WF

NN = (((1,), (0,)), ((), ()))
NT = (((1,), (1,)), ((), ()))
TN = (((0,), (0,)), ((), ()))


def mm(a, b, dims=NN, precision=None):
    return lax.dot_general(a, b, dims, precision=precision, preferred_element_type=F32)


def iota(shape, axis):
    return lax.broadcasted_iota(jnp.int32, shape, axis)


def gelu(x):
    return 0.5 * x * (1.0 + jnp.tanh(math.sqrt(2.0 / math.pi) * (x + 0.044715 * (x * x * x))))


def one_hot(condition):
    return jnp.where(condition, 1.0, 0.0).astype(BF16)


def band_weights(w_in, odd):
    shape = (5 * 128, DISP)
    row, col = iota(shape, 0), iota(shape, 1)
    lane = (row + 4) & 127
    dy = (row >> 7) * 2 + 1 - (lane >> 6) - odd
    dx = lane & 63
    hit = (dx < 9) & (dy >= 0) & (dy < 9) & (dy * 9 + dx == col)
    return (mm(one_hot(hit), w_in.astype(BF16), NT) * (1.0 / math.sqrt(D_FEAT))).astype(BF16)


def conv_weights(w_out_ref):
    zeros = jnp.zeros((2, DEC), F32)
    rows = []
    for kx in range(3):
        rows += [w_out_ref[ky, kx] for ky in range(3)] + [zeros]
    rows += [jnp.zeros((8, DEC), F32)]
    return jnp.concatenate(rows, axis=0).astype(BF16)


def mixing_weights(mix, frames, block):
    size = frames * block
    spread = one_hot(lax.div(iota((size, frames), 0), block) == iota((size, frames), 1))
    same = lax.rem(iota((size, size), 0), block) == lax.rem(iota((size, size), 1), block)
    high = mix.astype(BF16)
    low = (mix - high.astype(F32)).astype(BF16)
    parts = []
    for part in (high, low):
        rows = mm(spread, part).astype(BF16)
        parts.append(jnp.where(same, mm(rows, spread, NT), 0.0).astype(BF16))
    return parts


def hidden_rows(first_ref, first_at, next_ref, next_at, band_ref, bias, hid_ref):
    x, lane = 63 - iota((WF, 128), 0), (iota((WF, 128), 1) + 4) & 63
    inside = (lane < 9) & (x + lane >= 4) & (x + lane < WF + 4)
    row, col = iota((GROUP, GROUP), 0), iota((GROUP, GROUP), 1)
    turn = one_hot((row ^ 63) == col)

    def group(g, carry):
        at = pl.multiple_of(g * GROUP, GROUP)
        first = first_ref[pl.ds(first_at + at, GROUP), :]
        latter = next_ref[pl.ds(next_at + at, 3 * GROUP), :]
        products = mm(mm(turn, first).astype(BF16), latter, NT)
        for odd in range(2):
            pieces = []
            for i in (odd, odd + 2):
                blocks = []
                for m in range(i // 2, i // 2 + 5):
                    block = products[i * WF : (i + 1) * WF, m * 128 : (m + 1) * 128]
                    block = pltpu.roll(block, 1, 1, stride=1, stride_axis=0)
                    blocks.append(jnp.where(inside, block, 0.0).astype(BF16))
                pieces.append(jnp.concatenate(blocks, axis=1))
            skewed = jnp.concatenate(pieces, axis=0)
            hidden = gelu(mm(skewed, band_ref[odd]) + bias).astype(BF16)
            hidden = mm(turn[:128, :128], hidden).astype(BF16)
            hid_ref[pl.ds(at + odd * WF, WF), :] = hidden[:WF]
            hid_ref[pl.ds(at + (odd + 2) * WF, WF), :] = hidden[WF:]
        return carry

    lax.fori_loop(0, TASK // GROUP, group, 0)


def flow_rows(hid_ref, conv, base):
    taps = mm(conv, hid_ref[...], NT)
    lane = iota((8, TASK), 1) & 63
    across = (
        taps[8:16]
        + jnp.where(lane != 0, pltpu.roll(taps[0:8], 1, 1), 0.0)
        + jnp.where(lane != 63, pltpu.roll(taps[16:24], TASK - 1, 1), 0.0)
    )
    wide = TASK + 256
    across = jnp.concatenate([across, jnp.zeros((8, 256), F32)], axis=1)
    total = pltpu.roll(across, base + 64, 1)
    middle = pltpu.roll(across, base, 1) if base else across
    total = total + pltpu.roll(middle, 6, 0)
    total = total + pltpu.roll(pltpu.roll(across, (base + wide - 64) % wide, 1), 4, 0)
    return total[:, :STRIP]


def kernel(
    nx,
    nz,
    fa_ref,
    fb_ref,
    w_in_ref,
    b_in_ref,
    w_out_ref,
    mix_ref,
    ew_ref,
    eb_ref,
    flow_ref,
    grad_ref,
    a_buf,
    b_buf,
    rn_buf,
    rp_buf,
    band,
    conv,
    mixer,
    pooled,
    got1,
    got2,
    z_buf,
    zc_buf,
    zt_buf,
    mean0,
    mean_x,
    mean_y,
    mean1,
    mean_x2,
    mean_y2,
    mean2,
    mean_z,
    dev,
    send_1,
    recv_1,
    send_2,
    recv_2,
    send_3,
    recv_3,
    small,
    cov_z,
    cov_mid,
    cov_all,
    matrix,
    hid,
    strip_send,
    strip_recv,
    strip_own,
    grads,
    local_sem,
    send_sem,
    recv_sem,
):
    frames = nx * nx
    block = POOLED // frames
    rows = frames * block
    local_rows = 2 * rows
    lb = HALF // nx
    zr = lb // nz

    batch, t = lax.axis_index("batch"), lax.axis_index("tm")
    z, core = lax.div(batch, 2), lax.rem(batch, 2)
    x, y = lax.div(t, nx), lax.rem(t, nx)
    other = 1 - core

    def around(i, d, n):
        return lax.rem(i + d, n)

    x_peers = [(batch, around(x, d, nx) * nx + y) for d in range(1, nx)]
    y_peers = [(batch, x * nx + around(y, d, nx)) for d in range(1, nx)]
    z_peers = [(around(z, d, nz) * 2 + core, t) for d in range(1, nz)]
    partner = (z * 2 + other, t)
    y_partners = [(z * 2 + other, x * nx + around(y, d, nx)) for d in range(1, nx)]
    before = (batch, lax.rem(t + frames - 1, frames))
    after = (batch, lax.rem(t + 1, frames))

    count = [0]

    def remote(src, dst, device):
        i = count[0]
        count[0] += 1
        return pltpu.make_async_remote_copy(
            src_ref=src,
            dst_ref=dst,
            send_sem=send_sem.at[i],
            recv_sem=recv_sem.at[i],
            device_id=device,
            device_id_type=MESH,
        )

    def start(copies):
        for copy in copies:
            copy.start()
        started.extend(copies)

    def arrived(copies):
        for copy in copies:
            copy.wait_recv()

    started = []

    barrier = pltpu.get_barrier_semaphore()
    everyone = x_peers + y_peers + z_peers + [partner] + y_partners + [before, after]
    for device in everyone:
        pl.semaphore_signal(barrier, inc=1, device_id=device, device_id_type=MESH)

    load_a = pltpu.make_async_copy(fa_ref.at[0, 0], a_buf.at[pl.ds(REACH, POSITIONS)], local_sem.at[0])
    load_b = pltpu.make_async_copy(fb_ref.at[0, 0], b_buf, local_sem.at[1])
    load_a.start()
    load_b.start()

    a_buf[pl.ds(0, REACH), :] = jnp.zeros((REACH, D_FEAT), BF16)
    rn_buf[pl.ds(TASK + REACH, REACH), :] = jnp.zeros((REACH, D_FEAT), BF16)

    @pl.when(t == frames - 1)
    def _():
        rn_buf[pl.ds(0, TASK + REACH), :] = jnp.zeros((TASK + REACH, D_FEAT), BF16)

    @pl.when(t == 0)
    def _():
        rp_buf[...] = jnp.zeros((TASK, D_FEAT), BF16)

    mixer[0], mixer[1] = mixing_weights(mix_ref[...], frames, block)

    span = POSITIONS // frames
    prow, pcol = iota((block, span), 0), iota((block, span), 1)
    pooled_at = lax.div(pcol, GROUP) * 16 + lax.div(pcol & 63, 4)
    pool = one_hot(pooled_at == prow)
    load_a.wait()
    load_b.wait()

    def pool_block(k, carry):
        kx, ky = lax.div(k, nx), lax.rem(k, nx)
        at = pl.multiple_of(k * span, span)
        from_a = mm(pool, a_buf[pl.ds(REACH + at, span), :]) * (1.0 / 16.0)
        pooled[kx, ky, 0] = from_a.astype(BF16)
        from_b = mm(pool, b_buf[pl.ds(at, span), :]) * (1.0 / 16.0)
        pooled[kx, ky, 1] = from_b.astype(BF16)
        return carry

    lax.fori_loop(0, frames, pool_block, 0)
    pl.semaphore_wait(barrier, len(everyone))

    stage = [
        remote(pooled.at[around(x, d, nx)], got1.at[x], x_peers[d - 1]) for d in range(1, nx)
    ]
    start(stage)

    to_before = remote(
        a_buf.at[pl.ds(REACH + TASK - REACH, TASK + REACH)], rn_buf.at[pl.ds(0, TASK + REACH)], before
    )
    to_after = remote(a_buf.at[pl.ds(REACH, TASK)], rp_buf, after)

    @pl.when(t > 0)
    def _():
        to_before.start()

    @pl.when(t < frames - 1)
    def _():
        to_after.start()

    got1[x] = pooled[x]
    arrived(stage)
    stage = []
    for d in range(nx):
        for flip in range(2):
            if d == 0 and flip == 0:
                continue
            view = other if flip else core
            source = got1.at[:, around(y, d, nx), view]
            target = partner if d == 0 else (y_partners if flip else y_peers)[d - 1]
            stage.append(remote(source, got2.at[core, :, y], target))
    start(stage)
    got2[core, :, y] = got1[:, y, core]
    band[0] = band_weights(w_in_ref[...], 0)
    band[1] = band_weights(w_in_ref[...], 1)
    conv[...] = conv_weights(w_out_ref)
    arrived(stage)

    total = [jnp.zeros((1, 256), F32) for _ in range(EXP // 256)]
    for clip in range(2):
        features = got2[clip].reshape(rows, D_FEAT)
        mixed = (mm(mixer[0], features) + mm(mixer[1], features)).astype(BF16)
        for k in range(EXP // 256):
            cols = pl.ds(k * 256, 256)
            value = gelu(mm(mixed, ew_ref[:, cols]) + eb_ref[:, cols]).astype(BF16)
            z_buf[pl.ds(clip * rows, rows), cols] = value
            total[k] = total[k] + jnp.sum(value.astype(F32), axis=0, keepdims=True)
    mean = jnp.concatenate(total, axis=1) / local_rows
    mean0[0] = mean
    share_x = [remote(mean0.at[0], mean_x.at[d - 1], x_peers[d - 1]) for d in range(1, nx)]
    share_y = [remote(mean0.at[0], mean_y.at[d - 1], y_peers[d - 1]) for d in range(1, nx)]
    start(share_x)
    start(share_y)

    def center(k, carry):
        part = pl.ds(pl.multiple_of(k * 64, 64), 64)
        zc_buf[part, :] = (z_buf[part, :].astype(F32) - mean).astype(BF16)
        return carry

    lax.fori_loop(0, local_rows // 64, center, 0)
    for k in range(EXP // 256):
        zt_buf[pl.ds(k * 256, 256), :] = zc_buf[:, pl.ds(k * 256, 256)].T
    left, right = pl.ds(0, HALF), pl.ds(HALF, HALF)

    for k in range(HALF // 256):
        cols = pl.ds(HALF + k * 256, 256)
        cross = mm(zt_buf[left, :], zc_buf[:, cols]).astype(BF16)
        for j in range(256 // lb):
            send_1[0, k * (256 // lb) + j] = cross[:, j * lb : (j + 1) * lb]
    first_x = [
        remote(send_1.at[0, around(x, d, nx)], recv_1.at[0, d - 1], x_peers[d - 1])
        for d in range(1, nx)
    ]
    start(first_x)
    row_at, col_at = iota((HALF, 256), 0), iota((HALF, 256), 1)
    for k in range(HALF // 256):
        in_left = mm(zt_buf[left, :], zc_buf[:, pl.ds(k * 256, 256)])
        in_right = mm(zt_buf[right, :], zc_buf[:, pl.ds(HALF + k * 256, 256)])
        ahead = col_at + k * 256 - row_at
        both = jnp.where(ahead > 0, in_left, jnp.where(ahead < 0, in_right, 0.0)).astype(BF16)
        for j in range(256 // lb):
            send_1[1, k * (256 // lb) + j] = both[:, j * lb : (j + 1) * lb]
    first_y = [
        remote(send_1.at[1, around(y, d, nx)], recv_1.at[1, d - 1], y_peers[d - 1])
        for d in range(1, nx)
    ]
    start(first_y)

    def combine(own, parts, n):
        center = own
        for i in range(n - 1):
            center = center + parts[i]
        center = center / n
        lines = [own - center] + [parts[i] - center for i in range(n - 1)]
        lines += [jnp.zeros_like(own)] * (8 - n)
        dev[...] = jnp.concatenate(lines, axis=0)
        return center

    def outer(first_at, height, second_at):
        return mm(
            dev[:, pl.ds(first_at, height)],
            dev[:, pl.ds(second_at, lb)],
            TN,
            precision=lax.Precision.HIGHEST,
        )

    def triangles(first_at, height, block_at, inner_at):
        in_left = outer(first_at, height, block_at)
        in_right = outer(HALF + first_at, height, HALF + block_at)
        ahead = (block_at + iota((height, lb), 1)) - (inner_at + iota((height, lb), 0))
        return jnp.where(ahead > 0, in_left, jnp.where(ahead < 0, in_right, 0.0))

    x_at, y_at = pl.multiple_of(x * lb, lb), pl.multiple_of(y * lb, lb)

    arrived(share_x)
    center_x = combine(mean0[0], mean_x, nx)
    mean1[0] = center_x
    carry_x = [remote(mean1.at[0], mean_x2.at[d - 1], y_peers[d - 1]) for d in range(1, nx)]
    start(carry_x)
    part = local_rows * outer(0, HALF, HALF + x_at)
    arrived(first_x)
    part = part + send_1[0, x].astype(F32)
    for i in range(nx - 1):
        part = part + recv_1[0, i].astype(F32)
    send_2[0] = part.astype(BF16)
    second_x = [
        remote(
            send_2.at[0, pl.ds(pl.multiple_of(around(y, d, nx) * lb, lb), lb)],
            recv_2.at[0, d - 1],
            y_peers[d - 1],
        )
        for d in range(1, nx)
    ]
    start(second_x)

    arrived(share_y)
    center_y = combine(mean0[0], mean_y, nx)
    mean1[1] = center_y
    carry_y = [remote(mean1.at[1], mean_y2.at[d - 1], x_peers[d - 1]) for d in range(1, nx)]
    start(carry_y)
    part = local_rows * triangles(0, HALF, y_at, 0)
    arrived(first_y)
    part = part + send_1[1, y].astype(F32)
    for i in range(nx - 1):
        part = part + recv_1[1, i].astype(F32)
    send_2[1] = part.astype(BF16)
    second_y = [
        remote(
            send_2.at[1, pl.ds(pl.multiple_of(around(x, d, nx) * lb, lb), lb)],
            recv_2.at[1, d - 1],
            x_peers[d - 1],
        )
        for d in range(1, nx)
    ]
    start(second_y)

    arrived(carry_x)
    center_xy = combine(mean1[0], mean_x2, nx)
    mean2[0] = center_xy
    carry_z = [remote(mean2.at[0], mean_z.at[d - 1], z_peers[d - 1]) for d in range(1, nz)]
    start(carry_z)
    part = (local_rows * nx) * outer(y_at, lb, HALF + x_at)
    arrived(second_x)
    part = part + send_2[0, pl.ds(y_at, lb)].astype(F32)
    for i in range(nx - 1):
        part = part + recv_2[0, i].astype(F32)
    send_3[0] = part.astype(BF16)

    arrived(carry_y)
    combine(mean1[1], mean_y2, nx)
    part = (local_rows * nx) * triangles(x_at, lb, y_at, x_at)
    arrived(second_y)
    part = part + send_2[1, pl.ds(x_at, lb)].astype(F32)
    for i in range(nx - 1):
        part = part + recv_2[1, i].astype(F32)
    send_3[1] = part.astype(BF16)

    def z_rows(i):
        return pl.ds(pl.multiple_of(i * zr, zr), zr)

    third = [
        remote(send_3.at[:, z_rows(around(z, d, nz))], recv_3.at[d - 1], z_peers[d - 1])
        for d in range(1, nz)
    ]
    start(third)
    arrived(carry_z)
    mean = combine(mean2[0], mean_z, nz)
    group_rows = local_rows * frames
    small[0] = group_rows * outer(y_at, lb, HALF + x_at)
    small[1] = group_rows * triangles(x_at, lb, y_at, x_at)
    arrived(third)
    part = small[:, z_rows(z), :] + send_3[:, z_rows(z), :].astype(F32)
    for i in range(nz - 1):
        part = part + recv_3[i].astype(F32)
    scale = 1.0 / (group_rows * nz - 1) / math.sqrt(EXP)
    cov_z[:, z_rows(z), :] = (part * scale).astype(BF16)

    back_z = [
        remote(cov_z.at[:, z_rows(z)], cov_z.at[:, z_rows(z)], z_peers[d - 1])
        for d in range(1, nz)
    ]
    start(back_z)

    def center_all(k, carry):
        part = pl.ds(pl.multiple_of(k * 64, 64), 64)
        zc_buf[part, :] = (z_buf[part, :].astype(F32) - mean).astype(BF16)
        return carry

    lax.fori_loop(0, local_rows // 64, center_all, 0)
    arrived(back_z)
    y_rows, x_rows = pl.ds(y_at, lb), pl.ds(x_at, lb)
    back_2 = [
        remote(cov_z.at[0], cov_mid.at[0, y_rows], y_peers[d - 1]) for d in range(1, nx)
    ] + [remote(cov_z.at[1], cov_mid.at[1, x_rows], x_peers[d - 1]) for d in range(1, nx)]
    start(back_2)
    cov_mid[0, y_rows] = cov_z[0]
    cov_mid[1, x_rows] = cov_z[1]
    arrived(back_2)
    back_1 = [
        remote(cov_mid.at[0], cov_all.at[0, x], x_peers[d - 1]) for d in range(1, nx)
    ] + [remote(cov_mid.at[1], cov_all.at[1, y], y_peers[d - 1]) for d in range(1, nx)]
    start(back_1)
    cov_all[0, x] = cov_mid[0]
    cov_all[1, y] = cov_mid[1]

    bias = b_in_ref[...]

    @pl.when(t > 0)
    def _():
        to_after.wait_recv()

    hidden_rows(rp_buf, 0, a_buf, 0, band, bias, hid)
    strip_send[...] = flow_rows(hid, conv[...], 0)
    strip = remote(strip_send, strip_recv, before)
    start([strip])

    @pl.when(t < frames - 1)
    def _():
        to_before.wait_recv()

    hidden_rows(a_buf, REACH + TASK, rn_buf, 0, band, bias, hid)
    strip_own[...] = flow_rows(hid, conv[...], 128)

    arrived(back_1)
    pieces = HALF // lb
    cross = jnp.concatenate([cov_all[0, k] for k in range(pieces)], axis=1)
    both = jnp.concatenate([cov_all[1, k] for k in range(pieces)], axis=1)
    turned = both.T
    ahead = iota((HALF, HALF), 1) - iota((HALF, HALF), 0)
    matrix[left, right] = cross
    matrix[right, left] = cross.T
    matrix[left, left] = jnp.where(ahead > 0, both, turned)
    matrix[right, right] = jnp.where(ahead < 0, both, turned)

    def gradient(slot, clip):
        lines = pl.ds(pl.multiple_of(clip * rows, rows), rows)
        for k in range(EXP // 256):
            cols = pl.ds(k * 256, 256)
            grads[slot, :, cols] = mm(zc_buf[lines, :], matrix[:, cols]).astype(BF16)

    gradient(0, other)
    hand_over = remote(grads.at[0], grad_ref.at[core], partner)
    start([hand_over])
    gradient(1, core)
    keep = pltpu.make_async_copy(grads.at[1], grad_ref.at[core], local_sem.at[2])
    keep.start()

    arrived([strip])
    edge = STRIP - 256
    top, bottom = strip_recv[...], strip_own[...]
    flow_ref[:, 0:edge] = top[0:2, :edge]
    flow_ref[:, edge:STRIP] = top[0:2, edge:] + bottom[0:2, :256]
    flow_ref[:, STRIP:] = bottom[0:2, 256:]

    arrived([hand_over])
    keep.wait()

    @pl.when(t > 0)
    def _():
        to_before.wait_send()

    @pl.when(t < frames - 1)
    def _():
        to_after.wait_send()

    for copy in started:
        copy.wait_send()


def on_device(
    nx,
    nz,
    feat_a,
    feat_b,
    flow_in_weight,
    flow_entry_bias,
    flow_out_weight,
    frame_mix,
    expand_weight,
    expand_bias,
):
    frames = nx * nx
    block = POOLED // frames
    rows = frames * block
    lb = HALF // nx
    zr = lb // nz
    copies = 15 * (nx - 1) + 2 + nz * 3 + 8 + nx * 6
    vmem = pl.BlockSpec(memory_space=pltpu.VMEM)
    hbm = pl.BlockSpec(memory_space=pl.ANY)
    scratch = [
        pltpu.VMEM((REACH + POSITIONS, D_FEAT), BF16),
        pltpu.VMEM((POSITIONS, D_FEAT), BF16),
        pltpu.VMEM((NEXT_ROWS, D_FEAT), BF16),
        pltpu.VMEM((TASK, D_FEAT), BF16),
        pltpu.VMEM((2, 640, DEC), BF16),
        pltpu.VMEM((32, DEC), BF16),
        pltpu.VMEM((2, rows, rows), BF16),
        pltpu.VMEM((nx, nx, 2, block, D_FEAT), BF16),
        pltpu.VMEM((nx, nx, 2, block, D_FEAT), BF16),
        pltpu.VMEM((2, nx, nx, block, D_FEAT), BF16),
        pltpu.VMEM((2 * rows, EXP), BF16),
        pltpu.VMEM((2 * rows, EXP), BF16),
        pltpu.VMEM((EXP, 2 * rows), BF16),
        pltpu.VMEM((1, 1, EXP), F32),
        pltpu.VMEM((nx - 1, 1, EXP), F32),
        pltpu.VMEM((nx - 1, 1, EXP), F32),
        pltpu.VMEM((2, 1, EXP), F32),
        pltpu.VMEM((nx - 1, 1, EXP), F32),
        pltpu.VMEM((nx - 1, 1, EXP), F32),
        pltpu.VMEM((1, 1, EXP), F32),
        pltpu.VMEM((nz - 1, 1, EXP), F32),
        pltpu.VMEM((8, EXP), F32),
        pltpu.VMEM((2, nx, HALF, lb), BF16),
        pltpu.VMEM((2, nx - 1, HALF, lb), BF16),
        pltpu.VMEM((2, HALF, lb), BF16),
        pltpu.VMEM((2, nx - 1, lb, lb), BF16),
        pltpu.VMEM((2, lb, lb), BF16),
        pltpu.VMEM((nz - 1, 2, zr, lb), BF16),
        pltpu.VMEM((2, lb, lb), F32),
        pltpu.VMEM((2, lb, lb), BF16),
        pltpu.VMEM((2, HALF, lb), BF16),
        pltpu.VMEM((2, nx, HALF, lb), BF16),
        pltpu.VMEM((EXP, EXP), BF16),
        pltpu.VMEM((TASK, DEC), BF16),
        pltpu.VMEM((8, STRIP), F32),
        pltpu.VMEM((8, STRIP), F32),
        pltpu.VMEM((8, STRIP), F32),
        pltpu.VMEM((2, rows, EXP), BF16),
        pltpu.SemaphoreType.DMA((3,)),
        pltpu.SemaphoreType.DMA((copies,)),
        pltpu.SemaphoreType.DMA((copies,)),
    ]
    flow, grads = pl.pallas_call(
        functools.partial(kernel, nx, nz),
        out_shape=[
            jax.ShapeDtypeStruct((2, POSITIONS), F32),
            jax.ShapeDtypeStruct((2, rows, EXP), BF16),
        ],
        in_specs=[hbm, hbm] + [vmem] * 6,
        out_specs=[vmem, hbm],
        scratch_shapes=scratch,
        compiler_params=pltpu.CompilerParams(
            collective_id=0, has_side_effects=True, vmem_limit_bytes=56 * 1024 * 1024
        ),
    )(
        feat_a,
        feat_b,
        flow_in_weight,
        flow_entry_bias.reshape(1, DEC),
        flow_out_weight,
        frame_mix,
        expand_weight,
        expand_bias.reshape(1, EXP),
    )
    return (
        flow.reshape(1, 1, 2, POSITIONS),
        grads.reshape(2, 1, frames, block, EXP),
    )


def solution(mesh):
    nx = math.isqrt(mesh.shape["tm"])
    nz = mesh.shape["batch"] // 2
    return jax.shard_map(
        functools.partial(on_device, nx, nz),
        mesh=mesh,
        in_specs=(
            P("batch", "tm", None, None),
            P("batch", "tm", None, None),
            P(),
            P(),
            P(),
            P(),
            P(),
            P(),
        ),
        out_specs=(P("batch", "tm", None, None), P(None, "batch", None, "tm", None)),
        check_vma=False,
    )
```

time: 558 us -> 102 us (0.18); the launches traced: 550 us -> 101 us
  waiting for transfers between devices: 263 us -> 0 us
  Pallas kernels: 0 us -> 95.5 us
  matrix products: 94.9 us -> 0 us
  blocking collectives: 79 us -> 0 us
  local copies, waits for them, and re-layouts: 57.4 us -> 5.2 us
  other arithmetic: 22.9 us -> 0 us
  starting transfers between devices: 18.6 us -> 0 us
  between operations: 15 us -> 0.64 us
    unnamed x4 -> x0, waiting for transfers between devices: 131 us -> none
    psum x1 -> x0, waiting for transfers between devices: 106 us -> none  [on_device(): summed_block = lax.psum(partial_block, 'batch')]
    pallas_call x0 -> x1, Pallas kernels: none -> 95.5 us  [on_device(): pl.pallas_call(functools.partial(kernel, nx, nz), out_shape=[jax.ShapeDty...]
    dot_general x26 -> x0, matrix products: 94.9 us -> none  [the longest x9 32.5 us: banded_volume(): jnp.einsum('hxc,hyc->hxy', first, border_filled[shift:shift + HF], prefer...]
    psum x1 -> x0, blocking collectives: 79 us -> none  [on_device(): total_sums = lax.psum(local_sums, ('batch', 'tm'))]
    all_to_all x2 -> x0, waiting for transfers between devices: 26.1 us -> none  [the longest x1 22.4 us: on_device(): lax.all_to_all(pool_local(feat_a), 'tm', split_axis=2, concat_axis=1, til...]
    another operation x1 -> x0, local copies, waits for them, and re-layouts: 20.2 us -> none  [banded_volume(): jnp.stack([jnp.einsum('hxc,hyc->hxy', first, border_filled[shift:shift +...]
    all_to_all x2 -> x0, starting transfers between devices: 17 us -> none  [the longest x1 9.55 us: on_device(): lax.all_to_all(pool_local(feat_a), 'tm', split_axis=2, concat_axis=1, til...]
  transfers between devices with their start and end apart: 6 -> 0, of which waited for: 4 -> 0; matrix products, arithmetic and copies ran while one was open for 27% -> 0% of each run, Pallas kernels for 0% -> 0%
where the time goes in v1:
time: 102 us; the launch traced here: 101 us
  Pallas kernels  95.5 us (94%)
  local copies, waits for them, and re-layouts  5.2 us (5%)
    pallas_call x1, Pallas kernels, on_device(): pl.pallas_call(functools.partial(kernel, nx, nz), out_shape=[jax.ShapeDty...  95.5 us
    unnamed x3, local copies, waits for them, and re-layouts  5.2 us

profile of v1, /device:TPU:1, one launch (start us, length us, event | category | flops | bytes accessed | tf_op | source)
XLA Modules:
  0.0 101.3 jit_solution(11153652174010531061)
XLA Ops:
  0.6 1.5 %copy.10.w_in_ref = f32[128,81]{1,0:T(8,128)} copy(f32[128,81]{0,1:T(8,128)} %param.10) | data formatting | bytes 82944 | tf_op args[2]
  2.1 95.5 %shard_map.95 = (f32[2,4096]{1,0:T(2,128)}, bf16[2,256,1024]{2,1,0:T(8,128)(2,1)}) custom-call(bf16[1,1,4096,256]{3,2,1,0:T(8,128)(2,1)} %fa_ref.1, bf16[1,1,4096,256]{3,2,1,0:T(8,128)(2,1)} %fb_ref.1, f32[128,81]{1,0:T(8,128)} %copy.10.w_in_ref, f32[1,128]{1,0:T(1,128)} %bitcast.9, f32[3,3,2,128]{3,2,1,0:T(2,128)} %w_out_ref.1, f32[16,16]{1,0:T(8,128)} %mix_ref.1, ...), custom_call_target="tpu_custom_call" | custom-call | tf_op jit(solution)/shard_map/pallas_call | solution.py:625
  97.7 1.4 %copy.14 = f32[1,1,2,4096]{3,2,1,0:T(2,128)} copy(f32[1,1,2,4096]{3,2,1,0:T(2,128)} %bitcast.7) | data formatting | bytes 65536
  99.0 2.3 %copy.15 = bf16[2,1,16,16,1024]{4,3,2,1,0:T(8,128)(2,1)} copy(bf16[2,1,16,16,1024]{4,3,2,1,0:T(8,128)(2,1)} %bitcast.6) | data formatting | bytes 2097152

commit v2 on v1

--- a/solution.py
+++ b/solution.py
@@ -25,7 +25,19 @@
 TASK = 32 * WF
 REACH = 4 * WF
 NEXT_ROWS = TASK + 2 * REACH
+UNROLL = 2
 STRIP = 34 * WF
+
+SCHEDULE = {
+    "exchange": [("send", 0, 1)],
+    "embed": [("send", 1, 2)],
+    "first": [("upper", 0, 2), ("lower", 0, 1)],
+    "second": [("send", 2, 3), ("upper", 2, 4)],
+    "third": [("send", 3, 4), ("lower", 1, 3)],
+    "back z": [("upper", 4, 6)],
+    "back 2": [("lower", 3, 5)],
+    "back 1": [("upper", 6, 8), ("lower", 5, 8)],
+}
 
 NN = (((1,), (0,)), ((), ()))
 NT = (((1,), (1,)), ((), ()))
@@ -46,6 +58,11 @@
 
 def one_hot(condition):
     return jnp.where(condition, 1.0, 0.0).astype(BF16)
+
+
+def turn(size, kind):
+    hit = (iota((size, size), 0) ^ 63) == iota((size, size), 1)
+    return jnp.where(hit, 1.0, 0.0).astype(kind)
 
 
 def band_weights(w_in, odd):
@@ -55,13 +72,13 @@
     dy = (row >> 7) * 2 + 1 - (lane >> 6) - odd
     dx = lane & 63
     hit = (dx < 9) & (dy >= 0) & (dy < 9) & (dy * 9 + dx == col)
-    return (mm(one_hot(hit), w_in.astype(BF16), NT) * (1.0 / math.sqrt(D_FEAT))).astype(BF16)
+    return (mm(one_hot(hit), w_in.astype(BF16)) * (1.0 / math.sqrt(D_FEAT))).astype(BF16)
 
 
 def conv_weights(w_out_ref):
     zeros = jnp.zeros((2, DEC), F32)
     rows = []
-    for kx in range(3):
+    for kx in (2, 1, 0):
         rows += [w_out_ref[ky, kx] for ky in range(3)] + [zeros]
     rows += [jnp.zeros((8, DEC), F32)]
     return jnp.concatenate(rows, axis=0).astype(BF16)
@@ -80,17 +97,15 @@
     return parts
 
 
-def hidden_rows(first_ref, first_at, next_ref, next_at, band_ref, bias, hid_ref):
+def hidden_rows(low, high, first_ref, first_at, next_ref, next_at, band_ref, bias, hid_ref):
     x, lane = 63 - iota((WF, 128), 0), (iota((WF, 128), 1) + 4) & 63
     inside = (lane < 9) & (x + lane >= 4) & (x + lane < WF + 4)
-    row, col = iota((GROUP, GROUP), 0), iota((GROUP, GROUP), 1)
-    turn = one_hot((row ^ 63) == col)
 
     def group(g, carry):
         at = pl.multiple_of(g * GROUP, GROUP)
         first = first_ref[pl.ds(first_at + at, GROUP), :]
         latter = next_ref[pl.ds(next_at + at, 3 * GROUP), :]
-        products = mm(mm(turn, first).astype(BF16), latter, NT)
+        products = mm(first, latter, NT)
         for odd in range(2):
             pieces = []
             for i in (odd, odd + 2):
@@ -102,12 +117,11 @@
                 pieces.append(jnp.concatenate(blocks, axis=1))
             skewed = jnp.concatenate(pieces, axis=0)
             hidden = gelu(mm(skewed, band_ref[odd]) + bias).astype(BF16)
-            hidden = mm(turn[:128, :128], hidden).astype(BF16)
             hid_ref[pl.ds(at + odd * WF, WF), :] = hidden[:WF]
             hid_ref[pl.ds(at + (odd + 2) * WF, WF), :] = hidden[WF:]
         return carry
 
-    lax.fori_loop(0, TASK // GROUP, group, 0)
+    lax.fori_loop(low, high, group, 0, unroll=UNROLL)
 
 
 def flow_rows(hid_ref, conv, base):
@@ -124,7 +138,9 @@
     middle = pltpu.roll(across, base, 1) if base else across
     total = total + pltpu.roll(middle, 6, 0)
     total = total + pltpu.roll(pltpu.roll(across, (base + wide - 64) % wide, 1), 4, 0)
-    return total[:, :STRIP]
+    blocks = [total[:, k * 128 : (k + 1) * 128] for k in range(STRIP // 128)]
+    turned = mm(jnp.concatenate(blocks, axis=0), turn(128, F32), precision=lax.Precision.HIGHEST)
+    return jnp.concatenate([turned[k * 8 : (k + 1) * 8] for k in range(STRIP // 128)], axis=1)
 
 
 def kernel(
@@ -142,6 +158,7 @@
     grad_ref,
     a_buf,
     b_buf,
+    t_buf,
     rn_buf,
     rp_buf,
     band,
@@ -149,7 +166,7 @@
     mixer,
     pooled,
     got1,
-    got2,
+    got,
     z_buf,
     zc_buf,
     zt_buf,
@@ -272,45 +289,89 @@
     lax.fori_loop(0, frames, pool_block, 0)
     pl.semaphore_wait(barrier, len(everyone))
 
-    stage = [
+    exchange = [
         remote(pooled.at[around(x, d, nx)], got1.at[x], x_peers[d - 1]) for d in range(1, nx)
     ]
-    start(stage)
-
-    to_before = remote(
-        a_buf.at[pl.ds(REACH + TASK - REACH, TASK + REACH)], rn_buf.at[pl.ds(0, TASK + REACH)], before
-    )
-    to_after = remote(a_buf.at[pl.ds(REACH, TASK)], rp_buf, after)
-
-    @pl.when(t > 0)
-    def _():
-        to_before.start()
-
-    @pl.when(t < frames - 1)
-    def _():
-        to_after.start()
-
+    start(exchange)
+
+    turner = turn(GROUP, BF16)
+
+    def turn_group(k, carry):
+        at = pl.multiple_of(k * GROUP, GROUP)
+        turned = mm(turner, a_buf[pl.ds(REACH + at, GROUP), :])
+        t_buf[pl.ds(at, GROUP), :] = turned.astype(BF16)
+        return carry
+
+    lax.fori_loop(0, TASK // GROUP, turn_group, 0, unroll=4)
+
+    to_after, to_before = [], []
+    for c in range(4):
+        at, size = c * 8 * WF, 8 * WF
+        to_after.append(remote(t_buf.at[pl.ds(at, size)], rp_buf.at[pl.ds(at, size)], after))
+        at, size = (0, 12 * WF) if c == 0 else ((4 + 8 * c) * WF, 8 * WF)
+        to_before.append(remote(a_buf.at[pl.ds(TASK + at, size)], rn_buf.at[pl.ds(at, size)], before))
+
+    def not_first(action):
+        pl.when(t > 0)(action)
+
+    def not_last(action):
+        pl.when(t < frames - 1)(action)
+
+    bias = b_in_ref[...]
+    ready = set()
+    strips = []
+
+    def await_part(view, c):
+        if (view, c) not in ready:
+            ready.add((view, c))
+            if view == 0:
+                not_first(to_after[c].wait_recv)
+            else:
+                not_last(to_before[c].wait_recv)
+
+    def meanwhile(point):
+        for kind, low, high in SCHEDULE.get(point, ()):
+            if kind == "send":
+                for c in range(low, high):
+                    not_first(to_before[c].start)
+                    not_last(to_after[c].start)
+            elif kind == "upper":
+                for c in range((high + 1) // 2):
+                    await_part(0, c)
+                hidden_rows(low, high, rp_buf, 0, a_buf, 0, band, bias, hid.at[0])
+                if high == TASK // GROUP:
+                    strip_send[...] = flow_rows(hid.at[0], conv[...], 0)
+                    strips.append(remote(strip_send, strip_recv, before))
+                    start(strips)
+            else:
+                for c in range(min(3, high // 2) + 1):
+                    await_part(1, c)
+                hidden_rows(low, high, t_buf, TASK, rn_buf, 0, band, bias, hid.at[1])
+                if high == TASK // GROUP:
+                    strip_own[...] = flow_rows(hid.at[1], conv[...], 128)
+
+    meanwhile("exchange")
     got1[x] = pooled[x]
-    arrived(stage)
-    stage = []
+    arrived(exchange)
+    exchange = []
     for d in range(nx):
-        for flip in range(2):
-            if d == 0 and flip == 0:
-                continue
-            view = other if flip else core
-            source = got1.at[:, around(y, d, nx), view]
-            target = partner if d == 0 else (y_partners if flip else y_peers)[d - 1]
-            stage.append(remote(source, got2.at[core, :, y], target))
-    start(stage)
-    got2[core, :, y] = got1[:, y, core]
+        for view, targets in ((core, [None] + y_peers), (other, [partner] + y_partners)):
+            if targets[d] is not None:
+                source = got1.at[:, around(y, d, nx), view]
+                exchange.append(remote(source, got.at[core, :, y], targets[d]))
+    start(exchange)
+    meanwhile("exchange 2")
+    got[core, :, y] = got1[:, y, core]
+    lax.fori_loop(TASK // GROUP, 2 * (TASK // GROUP), turn_group, 0, unroll=4)
     band[0] = band_weights(w_in_ref[...], 0)
     band[1] = band_weights(w_in_ref[...], 1)
     conv[...] = conv_weights(w_out_ref)
-    arrived(stage)
+    arrived(exchange)
+    meanwhile("embed")
 
     total = [jnp.zeros((1, 256), F32) for _ in range(EXP // 256)]
     for clip in range(2):
-        features = got2[clip].reshape(rows, D_FEAT)
+        features = got[clip].reshape(rows, D_FEAT)
         mixed = (mm(mixer[0], features) + mm(mixer[1], features)).astype(BF16)
         for k in range(EXP // 256):
             cols = pl.ds(k * 256, 256)
@@ -357,6 +418,7 @@
         for d in range(1, nx)
     ]
     start(first_y)
+    meanwhile("first")
 
     def combine(own, parts, n):
         center = own
@@ -425,6 +487,7 @@
         for d in range(1, nx)
     ]
     start(second_y)
+    meanwhile("second")
 
     arrived(carry_x)
     center_xy = combine(mean1[0], mean_x2, nx)
@@ -455,6 +518,7 @@
         for d in range(1, nz)
     ]
     start(third)
+    meanwhile("third")
     arrived(carry_z)
     mean = combine(mean2[0], mean_z, nz)
     group_rows = local_rows * frames
@@ -479,6 +543,7 @@
         return carry
 
     lax.fori_loop(0, local_rows // 64, center_all, 0)
+    meanwhile("back z")
     arrived(back_z)
     y_rows, x_rows = pl.ds(y_at, lb), pl.ds(x_at, lb)
     back_2 = [
@@ -487,6 +552,7 @@
     start(back_2)
     cov_mid[0, y_rows] = cov_z[0]
     cov_mid[1, x_rows] = cov_z[1]
+    meanwhile("back 2")
     arrived(back_2)
     back_1 = [
         remote(cov_mid.at[0], cov_all.at[0, x], x_peers[d - 1]) for d in range(1, nx)
@@ -495,23 +561,7 @@
     cov_all[0, x] = cov_mid[0]
     cov_all[1, y] = cov_mid[1]
 
-    bias = b_in_ref[...]
-
-    @pl.when(t > 0)
-    def _():
-        to_after.wait_recv()
-
-    hidden_rows(rp_buf, 0, a_buf, 0, band, bias, hid)
-    strip_send[...] = flow_rows(hid, conv[...], 0)
-    strip = remote(strip_send, strip_recv, before)
-    start([strip])
-
-    @pl.when(t < frames - 1)
-    def _():
-        to_before.wait_recv()
-
-    hidden_rows(a_buf, REACH + TASK, rn_buf, 0, band, bias, hid)
-    strip_own[...] = flow_rows(hid, conv[...], 128)
+    meanwhile("back 1")
 
     arrived(back_1)
     pieces = HALF // lb
@@ -526,37 +576,54 @@
 
     def gradient(slot, clip):
         lines = pl.ds(pl.multiple_of(clip * rows, rows), rows)
-        for k in range(EXP // 256):
-            cols = pl.ds(k * 256, 256)
-            grads[slot, :, cols] = mm(zc_buf[lines, :], matrix[:, cols]).astype(BF16)
-
+        for k in range(2):
+            for j in range(2):
+                cols = pl.ds(k * HALF + j * 256, 256)
+                grads[slot, :, cols] = mm(zc_buf[lines, :], matrix[:, cols]).astype(BF16)
+            cols = pl.ds(k * HALF, HALF)
+            if slot == 0:
+                copy = remote(grads.at[0, :, cols], grad_ref.at[core, :, cols], partner)
+                start([copy])
+            else:
+                copy = pltpu.make_async_copy(
+                    grads.at[1, :, cols], grad_ref.at[core, :, cols], local_sem.at[2 + k]
+                )
+                copy.start()
+            results.append(copy)
+
+    results = []
     gradient(0, other)
-    hand_over = remote(grads.at[0], grad_ref.at[core], partner)
-    start([hand_over])
     gradient(1, core)
-    keep = pltpu.make_async_copy(grads.at[1], grad_ref.at[core], local_sem.at[2])
-    keep.start()
-
-    arrived([strip])
+
+    arrived(strips)
     edge = STRIP - 256
     top, bottom = strip_recv[...], strip_own[...]
     flow_ref[:, 0:edge] = top[0:2, :edge]
     flow_ref[:, edge:STRIP] = top[0:2, edge:] + bottom[0:2, :256]
     flow_ref[:, STRIP:] = bottom[0:2, 256:]
 
-    arrived([hand_over])
-    keep.wait()
-
-    @pl.when(t > 0)
-    def _():
-        to_before.wait_send()
-
-    @pl.when(t < frames - 1)
-    def _():
-        to_after.wait_send()
-
+    for copy in results:
+        copy.wait_recv()
+    for c in range(4):
+        not_first(to_before[c].wait_send)
+        not_last(to_after[c].wait_send)
     for copy in started:
         copy.wait_send()
+
+
+def hand_out(flow_in, grads_in, flow_out, grads_out, held, in_sem, out_sem):
+    loads, stores = [], []
+    for k in range(4):
+        part = (k // 2, pl.ds((k % 2) * 128, 128))
+        loads.append(pltpu.make_async_copy(grads_in.at[part], held.at[part], in_sem.at[k]))
+        stores.append(pltpu.make_async_copy(held.at[part], grads_out.at[part], out_sem.at[k]))
+        loads[k].start()
+    flow_out[...] = flow_in[...]
+    for k in range(4):
+        loads[k].wait()
+        stores[k].start()
+    for k in range(4):
+        stores[k].wait()
 
 
 def on_device(
@@ -576,11 +643,12 @@
     rows = frames * block
     lb = HALF // nx
     zr = lb // nz
-    copies = 15 * (nx - 1) + 2 + nz * 3 + 8 + nx * 6
+    copies = 3 * nx + 8 + 18 * (nx - 1) + 3 * (nz - 1) + 3
     vmem = pl.BlockSpec(memory_space=pltpu.VMEM)
     hbm = pl.BlockSpec(memory_space=pl.ANY)
     scratch = [
         pltpu.VMEM((REACH + POSITIONS, D_FEAT), BF16),
+        pltpu.VMEM((POSITIONS, D_FEAT), BF16),
         pltpu.VMEM((POSITIONS, D_FEAT), BF16),
         pltpu.VMEM((NEXT_ROWS, D_FEAT), BF16),
         pltpu.VMEM((TASK, D_FEAT), BF16),
@@ -613,12 +681,12 @@
         pltpu.VMEM((2, HALF, lb), BF16),
         pltpu.VMEM((2, nx, HALF, lb), BF16),
         pltpu.VMEM((EXP, EXP), BF16),
-        pltpu.VMEM((TASK, DEC), BF16),
+        pltpu.VMEM((2, TASK, DEC), BF16),
         pltpu.VMEM((8, STRIP), F32),
         pltpu.VMEM((8, STRIP), F32),
         pltpu.VMEM((8, STRIP), F32),
         pltpu.VMEM((2, rows, EXP), BF16),
-        pltpu.SemaphoreType.DMA((3,)),
+        pltpu.SemaphoreType.DMA((4,)),
         pltpu.SemaphoreType.DMA((copies,)),
         pltpu.SemaphoreType.DMA((copies,)),
     ]
@@ -637,13 +705,27 @@
     )(
         feat_a,
         feat_b,
-        flow_in_weight,
+        flow_in_weight.T,
         flow_entry_bias.reshape(1, DEC),
         flow_out_weight,
         frame_mix,
         expand_weight,
         expand_bias.reshape(1, EXP),
     )
+    flow, grads = pl.pallas_call(
+        hand_out,
+        out_shape=[
+            jax.ShapeDtypeStruct((2, POSITIONS), F32),
+            jax.ShapeDtypeStruct((2, rows, EXP), BF16),
+        ],
+        in_specs=[vmem, hbm],
+        out_specs=[vmem, hbm],
+        scratch_shapes=[
+            pltpu.VMEM((2, rows, EXP), BF16),
+            pltpu.SemaphoreType.DMA((4,)),
+            pltpu.SemaphoreType.DMA((4,)),
+        ],
+    )(flow, grads)
     return (
         flow.reshape(1, 1, 2, POSITIONS),
         grads.reshape(2, 1, frames, block, EXP),

time: 102 us -> 78.1 us (0.77)
  Pallas kernels: 95.5 us -> 77.1 us
  local copies, waits for them, and re-layouts: 5.2 us -> 0 us
    pallas_call x1, Pallas kernels: 95.5 us -> 73.8 us  [on_device(): pl.pallas_call(functools.partial(kernel, nx, nz), out_shape=[jax.ShapeDty...]
    unnamed x3 -> x0, local copies, waits for them, and re-layouts: 5.2 us -> none
    pallas_call x0 -> x1, Pallas kernels: none -> 3.35 us  [on_device(): pl.pallas_call(hand_out, out_shape=[jax.ShapeDtypeStruct((2, POSITIONS),...]
where the time goes in v2:
time: 78.1 us; the launch traced here: 77.9 us
  Pallas kernels  77.1 us (99%)
  between operations  0.8 us (1%)
    pallas_call x1, Pallas kernels, on_device(): pl.pallas_call(functools.partial(kernel, nx, nz), out_shape=[jax.ShapeDty...  73.8 us
    pallas_call x1, Pallas kernels, on_device(): pl.pallas_call(hand_out, out_shape=[jax.ShapeDtypeStruct((2, POSITIONS),...  3.35 us

profile of v2, /device:TPU:1, one launch (start us, length us, event | category | flops | bytes accessed | tf_op | source)
XLA Modules:
  0.0 77.9 jit_solution(4367981695640484787)
XLA Ops:
  0.6 73.8 %shard_map.95 = (f32[2,4096]{1,0:T(2,128)}, bf16[2,256,1024]{2,1,0:T(8,128)(2,1)}) custom-call(bf16[1,1,4096,256]{3,2,1,0:T(8,128)(2,1)} %fa_ref.1, bf16[1,1,4096,256]{3,2,1,0:T(8,128)(2,1)} %fb_ref.1, f32[81,128]{1,0:T(8,128)} %bitcast.7, f32[1,128]{1,0:T(1,128)} %bitcast.9, f32[3,3,2,128]{3,2,1,0:T(2,128)} %w_out_ref.1, f32[16,16]{1,0:T(8,128)} %mix_ref.1, ...), custom_call_target="tpu_custom_call" | custom-call | tf_op jit(solution)/shard_map/pallas_call | solution.py:693
  74.4 3.4 %shard_map.96 = (f32[2,4096]{1,0:T(2,128)}, bf16[2,256,1024]{2,1,0:T(8,128)(2,1)}) custom-call(f32[2,4096]{1,0:T(2,128)} %get-tuple-element.6.flow_in, bf16[2,256,1024]{2,1,0:T(8,128)(2,1)} %get-tuple-element.7.grads_in), custom_call_target="tpu_custom_call" | custom-call | tf_op jit(solution)/shard_map/pallas_call | solution.py:715

commit v3 on v2

--- a/solution.py
+++ b/solution.py
@@ -29,13 +29,12 @@
 STRIP = 34 * WF
 
 SCHEDULE = {
-    "exchange": [("send", 0, 1)],
-    "embed": [("send", 1, 2)],
-    "first": [("upper", 0, 2), ("lower", 0, 1)],
-    "second": [("send", 2, 3), ("upper", 2, 4)],
-    "third": [("send", 3, 4), ("lower", 1, 3)],
-    "back z": [("upper", 4, 6)],
-    "back 2": [("lower", 3, 5)],
+    "embed": [("send", 0, 1)],
+    "first": [("send", 1, 2)],
+    "second": [("send", 2, 3)],
+    "third": [("send", 3, 4), ("upper", 0, 2), ("lower", 0, 1)],
+    "back z": [("upper", 2, 4), ("lower", 1, 3)],
+    "back 2": [("upper", 4, 6), ("lower", 3, 5)],
     "back 1": [("upper", 6, 8), ("lower", 5, 8)],
 }
 
@@ -148,6 +147,14 @@
     nz,
     fa_ref,
     fb_ref,
+    w_in_any,
+    b_in_any,
+    w_out_any,
+    mix_any,
+    ew_any,
+    eb_any,
+    flow_any,
+    grad_ref,
     w_in_ref,
     b_in_ref,
     w_out_ref,
@@ -155,7 +162,6 @@
     ew_ref,
     eb_ref,
     flow_ref,
-    grad_ref,
     a_buf,
     b_buf,
     t_buf,
@@ -165,7 +171,6 @@
     conv,
     mixer,
     pooled,
-    got1,
     got,
     z_buf,
     zc_buf,
@@ -218,7 +223,6 @@
     y_peers = [(batch, x * nx + around(y, d, nx)) for d in range(1, nx)]
     z_peers = [(around(z, d, nz) * 2 + core, t) for d in range(1, nz)]
     partner = (z * 2 + other, t)
-    y_partners = [(z * 2 + other, x * nx + around(y, d, nx)) for d in range(1, nx)]
     before = (batch, lax.rem(t + frames - 1, frames))
     after = (batch, lax.rem(t + 1, frames))
 
@@ -248,14 +252,28 @@
     started = []
 
     barrier = pltpu.get_barrier_semaphore()
-    everyone = x_peers + y_peers + z_peers + [partner] + y_partners + [before, after]
-    for device in everyone:
+    for device in z_peers + [partner]:
         pl.semaphore_signal(barrier, inc=1, device_id=device, device_id_type=MESH)
 
+    def greet(d, carry):
+        for c in range(2):
+            device = (z * 2 + c, around(t, d, frames))
+            pl.semaphore_signal(barrier, inc=1, device_id=device, device_id_type=MESH)
+        return carry
+
+    lax.fori_loop(1, frames, greet, 0)
     load_a = pltpu.make_async_copy(fa_ref.at[0, 0], a_buf.at[pl.ds(REACH, POSITIONS)], local_sem.at[0])
     load_b = pltpu.make_async_copy(fb_ref.at[0, 0], b_buf, local_sem.at[1])
+    load_mix = pltpu.make_async_copy(mix_any, mix_ref, local_sem.at[4])
+    load_mix.start()
     load_a.start()
     load_b.start()
+    loads = []
+    for i, (source, target) in enumerate(
+        [(w_in_any, w_in_ref), (b_in_any, b_in_ref), (w_out_any, w_out_ref), (ew_any, ew_ref), (eb_any, eb_ref)]
+    ):
+        loads.append(pltpu.make_async_copy(source, target, local_sem.at[5 + i]))
+        loads[i].start()
 
     a_buf[pl.ds(0, REACH), :] = jnp.zeros((REACH, D_FEAT), BF16)
     rn_buf[pl.ds(TASK + REACH, REACH), :] = jnp.zeros((REACH, D_FEAT), BF16)
@@ -268,6 +286,7 @@
     def _():
         rp_buf[...] = jnp.zeros((TASK, D_FEAT), BF16)
 
+    load_mix.wait()
     mixer[0], mixer[1] = mixing_weights(mix_ref[...], frames, block)
 
     span = POSITIONS // frames
@@ -278,20 +297,24 @@
     load_b.wait()
 
     def pool_block(k, carry):
-        kx, ky = lax.div(k, nx), lax.rem(k, nx)
         at = pl.multiple_of(k * span, span)
         from_a = mm(pool, a_buf[pl.ds(REACH + at, span), :]) * (1.0 / 16.0)
-        pooled[kx, ky, 0] = from_a.astype(BF16)
+        pooled[k, 0] = from_a.astype(BF16)
         from_b = mm(pool, b_buf[pl.ds(at, span), :]) * (1.0 / 16.0)
-        pooled[kx, ky, 1] = from_b.astype(BF16)
+        pooled[k, 1] = from_b.astype(BF16)
         return carry
 
     lax.fori_loop(0, frames, pool_block, 0)
-    pl.semaphore_wait(barrier, len(everyone))
-
-    exchange = [
-        remote(pooled.at[around(x, d, nx)], got1.at[x], x_peers[d - 1]) for d in range(1, nx)
-    ]
+    for load in loads:
+        load.wait()
+    pl.semaphore_wait(barrier, nz - 1 + 1 + 2 * (frames - 1))
+
+    exchange = []
+    for d in range(frames):
+        to = around(t, d, frames)
+        for view, device in ((core, (batch, to)), (other, (z * 2 + other, to))):
+            if d > 0 or view is other:
+                exchange.append(remote(pooled.at[to, view], got.at[core, t], device))
     start(exchange)
 
     turner = turn(GROUP, BF16)
@@ -351,17 +374,7 @@
                     strip_own[...] = flow_rows(hid.at[1], conv[...], 128)
 
     meanwhile("exchange")
-    got1[x] = pooled[x]
-    arrived(exchange)
-    exchange = []
-    for d in range(nx):
-        for view, targets in ((core, [None] + y_peers), (other, [partner] + y_partners)):
-            if targets[d] is not None:
-                source = got1.at[:, around(y, d, nx), view]
-                exchange.append(remote(source, got.at[core, :, y], targets[d]))
-    start(exchange)
-    meanwhile("exchange 2")
-    got[core, :, y] = got1[:, y, core]
+    got[core, t] = pooled[t, core]
     lax.fori_loop(TASK // GROUP, 2 * (TASK // GROUP), turn_group, 0, unroll=4)
     band[0] = band_weights(w_in_ref[...], 0)
     band[1] = band_weights(w_in_ref[...], 1)
@@ -601,9 +614,12 @@
     flow_ref[:, 0:edge] = top[0:2, :edge]
     flow_ref[:, edge:STRIP] = top[0:2, edge:] + bottom[0:2, :256]
     flow_ref[:, STRIP:] = bottom[0:2, 256:]
+    store = pltpu.make_async_copy(flow_ref, flow_any, local_sem.at[10])
+    store.start()
 
     for copy in results:
         copy.wait_recv()
+    store.wait()
     for c in range(4):
         not_first(to_before[c].wait_send)
         not_last(to_after[c].wait_send)
@@ -611,19 +627,21 @@
         copy.wait_send()
 
 
-def hand_out(flow_in, grads_in, flow_out, grads_out, held, in_sem, out_sem):
+def hand_out(flow_in, grads_in, flow_out, grads_out, flow_held, held, in_sem, out_sem):
     loads, stores = [], []
     for k in range(4):
         part = (k // 2, pl.ds((k % 2) * 128, 128))
         loads.append(pltpu.make_async_copy(grads_in.at[part], held.at[part], in_sem.at[k]))
         stores.append(pltpu.make_async_copy(held.at[part], grads_out.at[part], out_sem.at[k]))
-        loads[k].start()
-    flow_out[...] = flow_in[...]
-    for k in range(4):
-        loads[k].wait()
-        stores[k].start()
-    for k in range(4):
-        stores[k].wait()
+    loads.append(pltpu.make_async_copy(flow_in, flow_held, in_sem.at[4]))
+    stores.append(pltpu.make_async_copy(flow_held, flow_out, out_sem.at[4]))
+    for load in loads:
+        load.start()
+    for load, store in zip(loads, stores):
+        load.wait()
+        store.start()
+    for store in stores:
+        store.wait()
 
 
 def on_device(
@@ -643,10 +661,16 @@
     rows = frames * block
     lb = HALF // nx
     zr = lb // nz
-    copies = 3 * nx + 8 + 18 * (nx - 1) + 3 * (nz - 1) + 3
-    vmem = pl.BlockSpec(memory_space=pltpu.VMEM)
+    copies = 2 * frames - 1 + 8 + 12 * (nx - 1) + 3 * (nz - 1) + 3
     hbm = pl.BlockSpec(memory_space=pl.ANY)
     scratch = [
+        pltpu.VMEM((DISP, DEC), F32),
+        pltpu.VMEM((1, DEC), F32),
+        pltpu.VMEM((3, 3, 2, DEC), F32),
+        pltpu.VMEM((frames, frames), F32),
+        pltpu.VMEM((D_FEAT, EXP), BF16),
+        pltpu.VMEM((1, EXP), F32),
+        pltpu.VMEM((2, POSITIONS), F32),
         pltpu.VMEM((REACH + POSITIONS, D_FEAT), BF16),
         pltpu.VMEM((POSITIONS, D_FEAT), BF16),
         pltpu.VMEM((POSITIONS, D_FEAT), BF16),
@@ -655,9 +679,8 @@
         pltpu.VMEM((2, 640, DEC), BF16),
         pltpu.VMEM((32, DEC), BF16),
         pltpu.VMEM((2, rows, rows), BF16),
-        pltpu.VMEM((nx, nx, 2, block, D_FEAT), BF16),
-        pltpu.VMEM((nx, nx, 2, block, D_FEAT), BF16),
-        pltpu.VMEM((2, nx, nx, block, D_FEAT), BF16),
+        pltpu.VMEM((frames, 2, block, D_FEAT), BF16),
+        pltpu.VMEM((2, frames, block, D_FEAT), BF16),
         pltpu.VMEM((2 * rows, EXP), BF16),
         pltpu.VMEM((2 * rows, EXP), BF16),
         pltpu.VMEM((EXP, 2 * rows), BF16),
@@ -686,7 +709,7 @@
         pltpu.VMEM((8, STRIP), F32),
         pltpu.VMEM((8, STRIP), F32),
         pltpu.VMEM((2, rows, EXP), BF16),
-        pltpu.SemaphoreType.DMA((4,)),
+        pltpu.SemaphoreType.DMA((11,)),
         pltpu.SemaphoreType.DMA((copies,)),
         pltpu.SemaphoreType.DMA((copies,)),
     ]
@@ -696,8 +719,8 @@
             jax.ShapeDtypeStruct((2, POSITIONS), F32),
             jax.ShapeDtypeStruct((2, rows, EXP), BF16),
         ],
-        in_specs=[hbm, hbm] + [vmem] * 6,
-        out_specs=[vmem, hbm],
+        in_specs=[hbm] * 8,
+        out_specs=[hbm, hbm],
         scratch_shapes=scratch,
         compiler_params=pltpu.CompilerParams(
             collective_id=0, has_side_effects=True, vmem_limit_bytes=56 * 1024 * 1024
@@ -718,12 +741,13 @@
             jax.ShapeDtypeStruct((2, POSITIONS), F32),
             jax.ShapeDtypeStruct((2, rows, EXP), BF16),
         ],
-        in_specs=[vmem, hbm],
-        out_specs=[vmem, hbm],
+        in_specs=[hbm, hbm],
+        out_specs=[hbm, hbm],
         scratch_shapes=[
+            pltpu.VMEM((2, POSITIONS), F32),
             pltpu.VMEM((2, rows, EXP), BF16),
-            pltpu.SemaphoreType.DMA((4,)),
-            pltpu.SemaphoreType.DMA((4,)),
+            pltpu.SemaphoreType.DMA((5,)),
+            pltpu.SemaphoreType.DMA((5,)),
         ],
     )(flow, grads)
     return (

time: 78.1 us -> 70.9 us (0.908)
  Pallas kernels: 77.1 us -> 70 us
    pallas_call x1, Pallas kernels: 73.8 us -> 68 us  [on_device(): pl.pallas_call(functools.partial(kernel, nx, nz), out_shape=[jax.ShapeDty...]
    pallas_call x1, Pallas kernels: 3.35 us -> 2 us  [on_device(): pl.pallas_call(hand_out, out_shape=[jax.ShapeDtypeStruct((2, POSITIONS),...]
where the time goes in v3:
time: 70.9 us; the launch traced here: 70.8 us
  Pallas kernels  70 us (99%)
  between operations  0.8 us (1%)
    pallas_call x1, Pallas kernels, on_device(): pl.pallas_call(functools.partial(kernel, nx, nz), out_shape=[jax.ShapeDty...  68 us
    pallas_call x1, Pallas kernels, on_device(): pl.pallas_call(hand_out, out_shape=[jax.ShapeDtypeStruct((2, POSITIONS),...  2 us

profile of v3, /device:TPU:1, one launch (start us, length us, event | category | flops | bytes accessed | tf_op | source)
XLA Modules:
  0.0 70.8 jit_solution(4958948074614974553)
XLA Ops:
  0.6 68.0 %shard_map.95 = (f32[2,4096]{1,0:T(2,128)}, bf16[2,256,1024]{2,1,0:T(8,128)(2,1)}) custom-call(bf16[1,1,4096,256]{3,2,1,0:T(8,128)(2,1)} %fa_ref.1, bf16[1,1,4096,256]{3,2,1,0:T(8,128)(2,1)} %fb_ref.1, f32[81,128]{1,0:T(8,128)} %bitcast.7, f32[1,128]{1,0:T(1,128)} %bitcast.9, f32[3,3,2,128]{3,2,1,0:T(2,128)} %w_out_any.1, f32[16,16]{1,0:T(8,128)} %mix_any.1, ...), custom_call_target="tpu_custom_call" | custom-call | tf_op jit(solution)/shard_map/pallas_call | solution.py:716
  68.6 2.0 %shard_map.96 = (f32[2,4096]{1,0:T(2,128)}, bf16[2,256,1024]{2,1,0:T(8,128)(2,1)}) custom-call(f32[2,4096]{1,0:T(2,128)} %get-tuple-element.6.flow_in, bf16[2,256,1024]{2,1,0:T(8,128)(2,1)} %get-tuple-element.7.grads_in), custom_call_target="tpu_custom_call" | custom-call | tf_op jit(solution)/shard_map/pallas_call | solution.py:738

commit v4 on v3

--- a/solution.py
+++ b/solution.py
@@ -32,10 +32,10 @@
     "embed": [("send", 0, 1)],
     "first": [("send", 1, 2)],
     "second": [("send", 2, 3)],
-    "third": [("send", 3, 4), ("upper", 0, 2), ("lower", 0, 1)],
-    "back z": [("upper", 2, 4), ("lower", 1, 3)],
-    "back 2": [("upper", 4, 6), ("lower", 3, 5)],
-    "back 1": [("upper", 6, 8), ("lower", 5, 8)],
+    "third": [("send", 3, 4), ("upper", 0, 2)],
+    "back z": [("upper", 2, 4), ("lower", 0, 2)],
+    "back 2": [("upper", 4, 6), ("lower", 2, 4)],
+    "back 1": [("upper", 6, 8), ("lower", 4, 8)],
 }
 
 NN = (((1,), (0,)), ((), ()))
@@ -201,6 +201,7 @@
     strip_own,
     grads,
     local_sem,
+    view_sem,
     send_sem,
     recv_sem,
 ):
@@ -262,12 +263,20 @@
         return carry
 
     lax.fori_loop(1, frames, greet, 0)
-    load_a = pltpu.make_async_copy(fa_ref.at[0, 0], a_buf.at[pl.ds(REACH, POSITIONS)], local_sem.at[0])
-    load_b = pltpu.make_async_copy(fb_ref.at[0, 0], b_buf, local_sem.at[1])
+    quarter = POSITIONS // 4
+    load_views = []
+    for k in range(4):
+        part = pl.ds(k * quarter, quarter)
+        load_views += [
+            pltpu.make_async_copy(
+                fa_ref.at[0, 0, part], a_buf.at[pl.ds(REACH + k * quarter, quarter)], view_sem.at[k]
+            ),
+            pltpu.make_async_copy(fb_ref.at[0, 0, part], b_buf.at[part], view_sem.at[4 + k]),
+        ]
     load_mix = pltpu.make_async_copy(mix_any, mix_ref, local_sem.at[4])
     load_mix.start()
-    load_a.start()
-    load_b.start()
+    for load in load_views:
+        load.start()
     loads = []
     for i, (source, target) in enumerate(
         [(w_in_any, w_in_ref), (b_in_any, b_in_ref), (w_out_any, w_out_ref), (ew_any, ew_ref), (eb_any, eb_ref)]
@@ -286,15 +295,10 @@
     def _():
         rp_buf[...] = jnp.zeros((TASK, D_FEAT), BF16)
 
-    load_mix.wait()
-    mixer[0], mixer[1] = mixing_weights(mix_ref[...], frames, block)
-
     span = POSITIONS // frames
     prow, pcol = iota((block, span), 0), iota((block, span), 1)
     pooled_at = lax.div(pcol, GROUP) * 16 + lax.div(pcol & 63, 4)
     pool = one_hot(pooled_at == prow)
-    load_a.wait()
-    load_b.wait()
 
     def pool_block(k, carry):
         at = pl.multiple_of(k * span, span)
@@ -304,9 +308,10 @@
         pooled[k, 1] = from_b.astype(BF16)
         return carry
 
-    lax.fori_loop(0, frames, pool_block, 0)
-    for load in loads:
-        load.wait()
+    for k in range(4):
+        load_views[2 * k].wait()
+        load_views[2 * k + 1].wait()
+        lax.fori_loop(k * frames // 4, (k + 1) * frames // 4, pool_block, 0, unroll=True)
     pl.semaphore_wait(barrier, nz - 1 + 1 + 2 * (frames - 1))
 
     exchange = []
@@ -331,7 +336,7 @@
     for c in range(4):
         at, size = c * 8 * WF, 8 * WF
         to_after.append(remote(t_buf.at[pl.ds(at, size)], rp_buf.at[pl.ds(at, size)], after))
-        at, size = (0, 12 * WF) if c == 0 else ((4 + 8 * c) * WF, 8 * WF)
+        at, size = c * 8 * WF, (12 if c == 3 else 8) * WF
         to_before.append(remote(a_buf.at[pl.ds(TASK + at, size)], rn_buf.at[pl.ds(at, size)], before))
 
     def not_first(action):
@@ -340,7 +345,6 @@
     def not_last(action):
         pl.when(t < frames - 1)(action)
 
-    bias = b_in_ref[...]
     ready = set()
     strips = []
 
@@ -367,7 +371,7 @@
                     strips.append(remote(strip_send, strip_recv, before))
                     start(strips)
             else:
-                for c in range(min(3, high // 2) + 1):
+                for c in range(min(3, (high + 1) // 2) + 1):
                     await_part(1, c)
                 hidden_rows(low, high, t_buf, TASK, rn_buf, 0, band, bias, hid.at[1])
                 if high == TASK // GROUP:
@@ -375,6 +379,11 @@
 
     meanwhile("exchange")
     got[core, t] = pooled[t, core]
+    load_mix.wait()
+    for load in loads:
+        load.wait()
+    bias = b_in_ref[...]
+    mixer[0], mixer[1] = mixing_weights(mix_ref[...], frames, block)
     lax.fori_loop(TASK // GROUP, 2 * (TASK // GROUP), turn_group, 0, unroll=4)
     band[0] = band_weights(w_in_ref[...], 0)
     band[1] = band_weights(w_in_ref[...], 1)
@@ -404,8 +413,11 @@
         return carry
 
     lax.fori_loop(0, local_rows // 64, center, 0)
-    for k in range(EXP // 256):
-        zt_buf[pl.ds(k * 256, 256), :] = zc_buf[:, pl.ds(k * 256, 256)].T
+    def transpose_columns(blocks):
+        for k in blocks:
+            zt_buf[pl.ds(k * 256, 256), :] = zc_buf[:, pl.ds(k * 256, 256)].T
+
+    transpose_columns(range(HALF // 256))
     left, right = pl.ds(0, HALF), pl.ds(HALF, HALF)
 
     for k in range(HALF // 256):
@@ -418,6 +430,7 @@
         for d in range(1, nx)
     ]
     start(first_x)
+    transpose_columns(range(HALF // 256, EXP // 256))
     row_at, col_at = iota((HALF, 256), 0), iota((HALF, 256), 1)
     for k in range(HALF // 256):
         in_left = mm(zt_buf[left, :], zc_buf[:, pl.ds(k * 256, 256)])
@@ -576,14 +589,15 @@
 
     meanwhile("back 1")
 
-    arrived(back_1)
     pieces = HALF // lb
+    arrived(back_1[: nx - 1])
     cross = jnp.concatenate([cov_all[0, k] for k in range(pieces)], axis=1)
+    matrix[left, right] = cross
+    matrix[right, left] = cross.T
+    arrived(back_1[nx - 1 :])
     both = jnp.concatenate([cov_all[1, k] for k in range(pieces)], axis=1)
     turned = both.T
     ahead = iota((HALF, HALF), 1) - iota((HALF, HALF), 0)
-    matrix[left, right] = cross
-    matrix[right, left] = cross.T
     matrix[left, left] = jnp.where(ahead > 0, both, turned)
     matrix[right, right] = jnp.where(ahead < 0, both, turned)
 
@@ -710,6 +724,7 @@
         pltpu.VMEM((8, STRIP), F32),
         pltpu.VMEM((2, rows, EXP), BF16),
         pltpu.SemaphoreType.DMA((11,)),
+        pltpu.SemaphoreType.DMA((8,)),
         pltpu.SemaphoreType.DMA((copies,)),
         pltpu.SemaphoreType.DMA((copies,)),
     ]

time: 70.9 us -> 68.3 us (0.963)
  Pallas kernels: 70 us -> 67.6 us
    pallas_call x1, Pallas kernels: 68 us -> 65.6 us  [on_device(): pl.pallas_call(functools.partial(kernel, nx, nz), out_shape=[jax.ShapeDty...]
where the time goes in v4:
time: 68.3 us; the launch traced here: 68.2 us
  Pallas kernels  67.6 us (99%)
    pallas_call x1, Pallas kernels, on_device(): pl.pallas_call(functools.partial(kernel, nx, nz), out_shape=[jax.ShapeDty...  65.6 us
    pallas_call x1, Pallas kernels, on_device(): pl.pallas_call(hand_out, out_shape=[jax.ShapeDtypeStruct((2, POSITIONS),...  2 us

profile of v4, /device:TPU:1, one launch (start us, length us, event | category | flops | bytes accessed | tf_op | source)
XLA Modules:
  0.0 68.2 jit_solution(5939556429489397887)
XLA Ops:
  0.6 65.6 %shard_map.95 = (f32[2,4096]{1,0:T(2,128)}, bf16[2,256,1024]{2,1,0:T(8,128)(2,1)}) custom-call(bf16[1,1,4096,256]{3,2,1,0:T(8,128)(2,1)} %fa_ref.1, bf16[1,1,4096,256]{3,2,1,0:T(8,128)(2,1)} %fb_ref.1, f32[81,128]{1,0:T(8,128)} %bitcast.7, f32[1,128]{1,0:T(1,128)} %bitcast.9, f32[3,3,2,128]{3,2,1,0:T(2,128)} %w_out_any.1, f32[16,16]{1,0:T(8,128)} %mix_any.1, ...), custom_call_target="tpu_custom_call" | custom-call | tf_op jit(solution)/shard_map/pallas_call | solution.py:731
  66.2 2.0 %shard_map.96 = (f32[2,4096]{1,0:T(2,128)}, bf16[2,256,1024]{2,1,0:T(8,128)(2,1)}) custom-call(f32[2,4096]{1,0:T(2,128)} %get-tuple-element.6.flow_in, bf16[2,256,1024]{2,1,0:T(8,128)(2,1)} %get-tuple-element.7.grads_in), custom_call_target="tpu_custom_call" | custom-call | tf_op jit(solution)/shard_map/pallas_call | solution.py:753

commit v5 on v4

--- a/solution.py
+++ b/solution.py
@@ -26,6 +26,7 @@
 REACH = 4 * WF
 NEXT_ROWS = TASK + 2 * REACH
 UNROLL = 2
+PARTS = 4
 STRIP = 34 * WF
 
 SCHEDULE = {
@@ -252,17 +253,6 @@
 
     started = []
 
-    barrier = pltpu.get_barrier_semaphore()
-    for device in z_peers + [partner]:
-        pl.semaphore_signal(barrier, inc=1, device_id=device, device_id_type=MESH)
-
-    def greet(d, carry):
-        for c in range(2):
-            device = (z * 2 + c, around(t, d, frames))
-            pl.semaphore_signal(barrier, inc=1, device_id=device, device_id_type=MESH)
-        return carry
-
-    lax.fori_loop(1, frames, greet, 0)
     quarter = POSITIONS // 4
     load_views = []
     for k in range(4):
@@ -284,17 +274,17 @@
         loads.append(pltpu.make_async_copy(source, target, local_sem.at[5 + i]))
         loads[i].start()
 
-    a_buf[pl.ds(0, REACH), :] = jnp.zeros((REACH, D_FEAT), BF16)
-    rn_buf[pl.ds(TASK + REACH, REACH), :] = jnp.zeros((REACH, D_FEAT), BF16)
-
-    @pl.when(t == frames - 1)
-    def _():
-        rn_buf[pl.ds(0, TASK + REACH), :] = jnp.zeros((TASK + REACH, D_FEAT), BF16)
-
-    @pl.when(t == 0)
-    def _():
-        rp_buf[...] = jnp.zeros((TASK, D_FEAT), BF16)
-
+    barrier = pltpu.get_barrier_semaphore()
+    for device in z_peers + [partner]:
+        pl.semaphore_signal(barrier, inc=1, device_id=device, device_id_type=MESH)
+
+    def greet(d, carry):
+        for c in range(2):
+            device = (z * 2 + c, around(t, d, frames))
+            pl.semaphore_signal(barrier, inc=1, device_id=device, device_id_type=MESH)
+        return carry
+
+    lax.fori_loop(1, frames, greet, 0)
     span = POSITIONS // frames
     prow, pcol = iota((block, span), 0), iota((block, span), 1)
     pooled_at = lax.div(pcol, GROUP) * 16 + lax.div(pcol & 63, 4)
@@ -333,10 +323,10 @@
     lax.fori_loop(0, TASK // GROUP, turn_group, 0, unroll=4)
 
     to_after, to_before = [], []
-    for c in range(4):
+    for c in range(PARTS):
         at, size = c * 8 * WF, 8 * WF
         to_after.append(remote(t_buf.at[pl.ds(at, size)], rp_buf.at[pl.ds(at, size)], after))
-        at, size = c * 8 * WF, (12 if c == 3 else 8) * WF
+        at, size = c * 8 * WF, (12 if c == PARTS - 1 else 8) * WF
         to_before.append(remote(a_buf.at[pl.ds(TASK + at, size)], rn_buf.at[pl.ds(at, size)], before))
 
     def not_first(action):
@@ -371,11 +361,22 @@
                     strips.append(remote(strip_send, strip_recv, before))
                     start(strips)
             else:
-                for c in range(min(3, (high + 1) // 2) + 1):
+                for c in range(min(PARTS, (high + 3) // 2)):
                     await_part(1, c)
                 hidden_rows(low, high, t_buf, TASK, rn_buf, 0, band, bias, hid.at[1])
                 if high == TASK // GROUP:
                     strip_own[...] = flow_rows(hid.at[1], conv[...], 128)
+
+    a_buf[pl.ds(0, REACH), :] = jnp.zeros((REACH, D_FEAT), BF16)
+    rn_buf[pl.ds(TASK + REACH, REACH), :] = jnp.zeros((REACH, D_FEAT), BF16)
+
+    @pl.when(t == frames - 1)
+    def _():
+        rn_buf[pl.ds(0, TASK + REACH), :] = jnp.zeros((TASK + REACH, D_FEAT), BF16)
+
+    @pl.when(t == 0)
+    def _():
+        rp_buf[...] = jnp.zeros((TASK, D_FEAT), BF16)
 
     meanwhile("exchange")
     got[core, t] = pooled[t, core]
@@ -404,15 +405,14 @@
     mean0[0] = mean
     share_x = [remote(mean0.at[0], mean_x.at[d - 1], x_peers[d - 1]) for d in range(1, nx)]
     share_y = [remote(mean0.at[0], mean_y.at[d - 1], y_peers[d - 1]) for d in range(1, nx)]
-    start(share_x)
-    start(share_y)
 
     def center(k, carry):
         part = pl.ds(pl.multiple_of(k * 64, 64), 64)
         zc_buf[part, :] = (z_buf[part, :].astype(F32) - mean).astype(BF16)
         return carry
 
-    lax.fori_loop(0, local_rows // 64, center, 0)
+    lax.fori_loop(0, local_rows // 64, center, 0, unroll=2)
+
     def transpose_columns(blocks):
         for k in blocks:
             zt_buf[pl.ds(k * 256, 256), :] = zc_buf[:, pl.ds(k * 256, 256)].T
@@ -420,16 +420,6 @@
     transpose_columns(range(HALF // 256))
     left, right = pl.ds(0, HALF), pl.ds(HALF, HALF)
 
-    for k in range(HALF // 256):
-        cols = pl.ds(HALF + k * 256, 256)
-        cross = mm(zt_buf[left, :], zc_buf[:, cols]).astype(BF16)
-        for j in range(256 // lb):
-            send_1[0, k * (256 // lb) + j] = cross[:, j * lb : (j + 1) * lb]
-    first_x = [
-        remote(send_1.at[0, around(x, d, nx)], recv_1.at[0, d - 1], x_peers[d - 1])
-        for d in range(1, nx)
-    ]
-    start(first_x)
     transpose_columns(range(HALF // 256, EXP // 256))
     row_at, col_at = iota((HALF, 256), 0), iota((HALF, 256), 1)
     for k in range(HALF // 256):
@@ -444,6 +434,18 @@
         for d in range(1, nx)
     ]
     start(first_y)
+    for k in range(HALF // 256):
+        cols = pl.ds(HALF + k * 256, 256)
+        cross = mm(zt_buf[left, :], zc_buf[:, cols]).astype(BF16)
+        for j in range(256 // lb):
+            send_1[0, k * (256 // lb) + j] = cross[:, j * lb : (j + 1) * lb]
+    first_x = [
+        remote(send_1.at[0, around(x, d, nx)], recv_1.at[0, d - 1], x_peers[d - 1])
+        for d in range(1, nx)
+    ]
+    start(first_x)
+    start(share_x)
+    start(share_y)
     meanwhile("first")
 
     def combine(own, parts, n):
@@ -634,7 +636,7 @@
     for copy in results:
         copy.wait_recv()
     store.wait()
-    for c in range(4):
+    for c in range(PARTS):
         not_first(to_before[c].wait_send)
         not_last(to_after[c].wait_send)
     for copy in started:
@@ -675,7 +677,7 @@
     rows = frames * block
     lb = HALF // nx
     zr = lb // nz
-    copies = 2 * frames - 1 + 8 + 12 * (nx - 1) + 3 * (nz - 1) + 3
+    copies = 2 * frames - 1 + 2 * PARTS + 12 * (nx - 1) + 3 * (nz - 1) + 3
     hbm = pl.BlockSpec(memory_space=pl.ANY)
     scratch = [
         pltpu.VMEM((DISP, DEC), F32),

time: 68.3 us -> 68.4 us (level)
  no operation moved by 1% of the time
where the time goes in v5:
time: 68.4 us; the launch traced here: 68.3 us
  Pallas kernels  67.6 us (99%)
    pallas_call x1, Pallas kernels, on_device(): pl.pallas_call(functools.partial(kernel, nx, nz), out_shape=[jax.ShapeDty...  65.6 us
    pallas_call x1, Pallas kernels, on_device(): pl.pallas_call(hand_out, out_shape=[jax.ShapeDtypeStruct((2, POSITIONS),...  2 us

profile of v5, /device:TPU:1, one launch (start us, length us, event | category | flops | bytes accessed | tf_op | source)
XLA Modules:
  0.0 68.3 jit_solution(4656859462984730000)
XLA Ops:
  0.6 65.6 %shard_map.95 = (f32[2,4096]{1,0:T(2,128)}, bf16[2,256,1024]{2,1,0:T(8,128)(2,1)}) custom-call(bf16[1,1,4096,256]{3,2,1,0:T(8,128)(2,1)} %fa_ref.1, bf16[1,1,4096,256]{3,2,1,0:T(8,128)(2,1)} %fb_ref.1, f32[81,128]{1,0:T(8,128)} %bitcast.7, f32[1,128]{1,0:T(1,128)} %bitcast.9, f32[3,3,2,128]{3,2,1,0:T(2,128)} %w_out_any.1, f32[16,16]{1,0:T(8,128)} %mix_any.1, ...), custom_call_target="tpu_custom_call" | custom-call | tf_op jit(solution)/shard_map/pallas_call | solution.py:733
  66.3 2.0 %shard_map.96 = (f32[2,4096]{1,0:T(2,128)}, bf16[2,256,1024]{2,1,0:T(8,128)(2,1)}) custom-call(f32[2,4096]{1,0:T(2,128)} %get-tuple-element.6.flow_in, bf16[2,256,1024]{2,1,0:T(8,128)(2,1)} %get-tuple-element.7.grads_in), custom_call_target="tpu_custom_call" | custom-call | tf_op jit(solution)/shard_map/pallas_call | solution.py:755

commit v6 on v5

--- a/solution.py
+++ b/solution.py
@@ -605,17 +605,15 @@
 
     def gradient(slot, clip):
         lines = pl.ds(pl.multiple_of(clip * rows, rows), rows)
-        for k in range(2):
-            for j in range(2):
-                cols = pl.ds(k * HALF + j * 256, 256)
-                grads[slot, :, cols] = mm(zc_buf[lines, :], matrix[:, cols]).astype(BF16)
-            cols = pl.ds(k * HALF, HALF)
+        for k in range(4):
+            cols = pl.ds(k * 256, 256)
+            grads[slot, :, cols] = mm(zc_buf[lines, :], matrix[:, cols]).astype(BF16)
             if slot == 0:
                 copy = remote(grads.at[0, :, cols], grad_ref.at[core, :, cols], partner)
                 start([copy])
             else:
                 copy = pltpu.make_async_copy(
-                    grads.at[1, :, cols], grad_ref.at[core, :, cols], local_sem.at[2 + k]
+                    grads.at[1, :, cols], grad_ref.at[core, :, cols], local_sem.at[(0, 1, 2, 3)[k]]
                 )
                 copy.start()
             results.append(copy)
@@ -677,7 +675,7 @@
     rows = frames * block
     lb = HALF // nx
     zr = lb // nz
-    copies = 2 * frames - 1 + 2 * PARTS + 12 * (nx - 1) + 3 * (nz - 1) + 3
+    copies = 2 * frames - 1 + 2 * PARTS + 12 * (nx - 1) + 3 * (nz - 1) + 5
     hbm = pl.BlockSpec(memory_space=pl.ANY)
     scratch = [
         pltpu.VMEM((DISP, DEC), F32),

time: 68.4 us -> 69 us (level)
  no operation moved by 1% of the time
where the time goes in v6:
time: 69 us; the launch traced here: 68.9 us
  Pallas kernels  68.1 us (99%)
  between operations  0.8 us (1%)
    pallas_call x1, Pallas kernels, on_device(): pl.pallas_call(functools.partial(kernel, nx, nz), out_shape=[jax.ShapeDty...  66.1 us
    pallas_call x1, Pallas kernels, on_device(): pl.pallas_call(hand_out, out_shape=[jax.ShapeDtypeStruct((2, POSITIONS),...  2 us

profile of v6, /device:TPU:1, one launch (start us, length us, event | category | flops | bytes accessed | tf_op | source)
XLA Modules:
  0.0 68.9 jit_solution(4541284921941298534)
XLA Ops:
  0.6 66.1 %shard_map.95 = (f32[2,4096]{1,0:T(2,128)}, bf16[2,256,1024]{2,1,0:T(8,128)(2,1)}) custom-call(bf16[1,1,4096,256]{3,2,1,0:T(8,128)(2,1)} %fa_ref.1, bf16[1,1,4096,256]{3,2,1,0:T(8,128)(2,1)} %fb_ref.1, f32[81,128]{1,0:T(8,128)} %bitcast.7, f32[1,128]{1,0:T(1,128)} %bitcast.9, f32[3,3,2,128]{3,2,1,0:T(2,128)} %w_out_any.1, f32[16,16]{1,0:T(8,128)} %mix_any.1, ...), custom_call_target="tpu_custom_call" | custom-call | tf_op jit(solution)/shard_map/pallas_call | solution.py:731
  66.8 2.0 %shard_map.96 = (f32[2,4096]{1,0:T(2,128)}, bf16[2,256,1024]{2,1,0:T(8,128)(2,1)}) custom-call(f32[2,4096]{1,0:T(2,128)} %get-tuple-element.6.flow_in, bf16[2,256,1024]{2,1,0:T(8,128)(2,1)} %get-tuple-element.7.grads_in), custom_call_target="tpu_custom_call" | custom-call | tf_op jit(solution)/shard_map/pallas_call | solution.py:753
